TPU v7x, 32 devices: a whole 2x2x4 slice. The times are simulated.
32 devices in a mesh: seq: 32 (over z, y, x, core), mp: 1.
Axes of the slice: x: 2, y: 2, z: 4, core: 2. Of those that a mesh axis runs over, the one named last changes fastest.
Arguments:
- states: bfloat16 [8192, 2560], P('seq'), may hold values from -8 to 8
- query_rows: bfloat16 [8192, 1280], P('seq', 'mp'), may hold values from -8 to 8
- key_rows: bfloat16 [8192, 1280], P('seq', 'mp'), may hold values from -8 to 8
- value_rows: bfloat16 [8192, 1280], P('seq', 'mp'), may hold values from -6 to 6
- out_proj: bfloat16 [1280, 2560], P('mp'), may hold values from -0.15625 to 0.15625
- norm_gain: float32 [2560], replicated, may hold values from 0.1 to 1.9
- up_proj: bfloat16 [2560, 5120], P(None, 'mp'), may hold values from -0.125 to 0.125
- down_proj: bfloat16 [5120, 2560], P('mp', 'seq'), may hold values from -0.078125 to 0.078125
Outputs:
- layer_out: bfloat16 [8192, 2560], P('seq', 'mp')
All inputs are finite; a program needn't handle non-finite values.
Results may differ from a plain program's by a relative error of at most 0.008.
Values may be sent and summed in bfloat16 or wider, within the bound.
A program may use at most 192 MiB of HBM per device.

v0:
```python
import jax
import jax.numpy as jnp
from jax import lax
from jax.sharding import PartitionSpec as P

HEAD_DIM = 80
SEG0 = 2048


def swapped(shard, axis, distance):
    return lax.ppermute(shard, axis, [(i, i ^ 1 << distance) for i in range(lax.axis_size(axis))])


def select_rows(source, stride, offsets):
    leading = source.shape[:-2]
    row_count, col_count = (source.shape[-2], source.shape[-1])
    grouped = source.reshape(leading + (row_count // stride, stride, col_count))
    picked = jnp.arange(stride)[:, None] == offsets[None, :]
    return jnp.sum(jnp.where(picked, grouped, jnp.zeros((), source.dtype)), axis=-2)


def spread_rows(source, stride, offsets):
    row_count, col_count = source.shape
    picked = jnp.arange(stride)[:, None] == offsets[None, :]
    placed = jnp.where(picked[None], source[:, None, :], jnp.zeros((), source.dtype))
    return placed.reshape(row_count * stride, col_count)


def join_halves(mine, other, seq_pos, bit_pos):
    upper = seq_pos // 2**bit_pos % 2 == 1
    return jnp.where(
        upper, jnp.concatenate([other, mine], axis=-2), jnp.concatenate([mine, other], axis=-2)
    )


def tier_attend(query_sel, packed, first_row):
    query_count, col_count = query_sel.shape
    key_count = packed.shape[1]
    head_count = col_count // HEAD_DIM
    query_heads = query_sel.reshape(query_count, head_count, HEAD_DIM)
    key_heads = packed[0].reshape(key_count, head_count, HEAD_DIM)
    value_heads = packed[1].reshape(key_count, head_count, HEAD_DIM)
    scores = jnp.einsum(
        "qhd,khd->hqk", query_heads, key_heads, preferred_element_type=jnp.float32
    ) * HEAD_DIM ** (-0.5)
    allowed = jnp.arange(key_count)[None, :] <= (first_row + jnp.arange(query_count))[:, None]
    scores = jnp.where(allowed[None], scores, -1e30)
    row_peak = jnp.max(scores, axis=-1)
    shifted_exp = jnp.exp(scores - row_peak[..., None])
    row_total = jnp.sum(shifted_exp, axis=-1)
    weighted = jnp.einsum(
        "hqk,khd->qhd",
        shifted_exp.astype(jnp.bfloat16),
        value_heads,
        preferred_element_type=jnp.float32,
    )
    return (row_peak.T, row_total.T, weighted.reshape(query_count, col_count))


def per_device(states, query_rows, key_rows, value_rows, out_proj, norm_gain, up_proj, down_proj):
    tok_dev, col_count = query_rows.shape
    local_heads = col_count // HEAD_DIM
    model_width = states.shape[1]
    seq_count = lax.axis_size("seq")
    seq_pos = lax.axis_index("seq")
    mp_pos = lax.axis_index("mp")
    total_rows = tok_dev * seq_count
    col_heads = mp_pos * local_heads + jnp.arange(col_count) // HEAD_DIM
    head_ids = mp_pos * local_heads + jnp.arange(local_heads)
    tier_count = 0
    while SEG0 * 2**tier_count <= total_rows and total_rows % (SEG0 * 2**tier_count) == 0:
        tier_count += 1
    base_bits = (SEG0 // tok_dev).bit_length() - 1
    buffers = []
    for tier_idx in range(tier_count):
        stride = 2**tier_idx
        packed = jnp.stack(
            [
                select_rows(key_rows, stride, col_heads % stride),
                select_rows(value_rows, stride, col_heads % stride),
            ]
        )
        for bit_pos in range(base_bits + tier_idx):
            packed = join_halves(packed, swapped(packed, "seq", bit_pos), seq_pos, bit_pos)
        buffers.append(packed)
    run_peak, run_total, run_acc = (None, None, None)
    for tier_idx in range(tier_count):
        stride = 2**tier_idx
        query_sel = select_rows(query_rows, stride, col_heads % stride)
        group_devs = SEG0 * stride // tok_dev
        first_row = seq_pos % group_devs * (tok_dev // stride)
        tier_peak, tier_total, tier_sum = tier_attend(query_sel, buffers[tier_idx], first_row)
        head_offsets = head_ids % stride
        full_peak = spread_rows(tier_peak, stride, head_offsets)
        full_total = spread_rows(tier_total, stride, head_offsets)
        full_sum = spread_rows(tier_sum, stride, col_heads % stride)
        if tier_idx == 0:
            run_peak, run_total, run_acc = (full_peak, full_total, full_sum)
        else:
            chosen = spread_rows(jnp.ones_like(tier_peak), stride, head_offsets) > 0.5
            candidate = jnp.where(chosen, full_peak, run_peak)
            new_peak = jnp.maximum(run_peak, candidate)
            keep_old = jnp.exp(run_peak - new_peak)
            take_new = jnp.where(chosen, jnp.exp(candidate - new_peak), 0.0)
            run_total = keep_old * run_total + take_new * full_total
            run_acc = (
                jnp.repeat(keep_old, HEAD_DIM, axis=1) * run_acc
                + jnp.repeat(take_new, HEAD_DIM, axis=1) * full_sum
            )
            run_peak = new_peak
    attended = (run_acc / jnp.repeat(run_total, HEAD_DIM, axis=1)).astype(jnp.bfloat16)
    projected = jnp.dot(attended, out_proj, preferred_element_type=jnp.float32)
    share = lax.psum_scatter(projected, "mp", scatter_dimension=1, tiled=True)
    half_width = share.shape[1]
    states_share = lax.dynamic_slice_in_dim(states, mp_pos * half_width, half_width, 1)
    resid_share = (states_share.astype(jnp.float32) + share).astype(jnp.bfloat16)
    share_wide = resid_share.astype(jnp.float32)
    part_sum, part_squares = lax.psum(
        (
            jnp.sum(share_wide, axis=1, keepdims=True),
            jnp.sum(share_wide * share_wide, axis=1, keepdims=True),
        ),
        "mp",
    )
    row_mean = part_sum / model_width
    row_var = part_squares / model_width - row_mean * row_mean
    gain_share = lax.dynamic_slice_in_dim(norm_gain, mp_pos * half_width, half_width, 0)
    normed_share = (
        (share_wide - row_mean) * lax.rsqrt(row_var + 1e-05) * gain_share[None, :]
    ).astype(jnp.bfloat16)
    normed = lax.all_gather(normed_share, "mp", axis=1, tiled=True)
    hidden = jax.nn.gelu(
        jnp.dot(normed, up_proj, preferred_element_type=jnp.float32), approximate=False
    ).astype(jnp.bfloat16)
    down_whole = lax.all_gather(down_proj, "seq", axis=1, tiled=True)
    terms = jnp.dot(hidden, down_whole, preferred_element_type=jnp.float32)
    ffn_part = lax.psum_scatter(
        terms.astype(jnp.bfloat16), "mp", scatter_dimension=1, tiled=True
    ).astype(jnp.float32)
    return (resid_share.astype(jnp.float32) + ffn_part).astype(jnp.bfloat16)


def solution(mesh):
    in_specs = (
        P("seq", None),
        P("seq", "mp"),
        P("seq", "mp"),
        P("seq", "mp"),
        P("mp", None),
        P(),
        P(None, "mp"),
        P("mp", "seq"),
    )
    out_specs = P("seq", "mp")
    return jax.shard_map(
        per_device, mesh=mesh, in_specs=in_specs, out_specs=out_specs, check_vma=False
    )
```

profile of v0, /device:TPU:24, one launch (start us, length us, event | category | flops | bytes accessed | tf_op | source)
XLA Modules:
  0.0 781.0 jit_solution(9077991795885342688)
XLA Ops:
  25.3 5.8 fusion.94
  35.5 90.9 %collective-permute-done.8 = bf16[2,128,1280]{2,1,0:T(8,128)(2,1)} collective-permute-done((bf16[2,128,1280]{2,1,0:T(8,128)(2,1)S(1)}, bf16[2,128,1280]{2,1,0:T(8,128)(2,1)}, u32[]{:S(2)}, u32[]{:S(2)}) %collective-permute-start.8) | collective-permute-done | bytes 655392 | tf_op jit(solution)/shard_map/ppermute | solution.py:11
  130.6 7.2 maximum_select_fusion.3
  138.4 44.0 %collective-permute-done.4 = bf16[2,256,1280]{2,1,0:T(8,128)(2,1)S(1)} collective-permute-done((bf16[2,256,1280]{2,1,0:T(8,128)(2,1)S(1)}, bf16[2,256,1280]{2,1,0:T(8,128)(2,1)S(1)}, u32[]{:S(2)}, u32[]{:S(2)}) %collective-permute-start.4) | collective-permute-done | bytes 1310752 | tf_op jit(solution)/shard_map/ppermute | solution.py:11
  185.1 4.0 collective-permute-done.9
  189.1 4.5 maximum_select_fusion.8
  201.2 160.1 %collective-permute-done.5 = bf16[2,512,1280]{2,1,0:T(8,128)(2,1)} collective-permute-done((bf16[2,512,1280]{2,1,0:T(8,128)(2,1)S(1)}, bf16[2,512,1280]{2,1,0:T(8,128)(2,1)}, u32[]{:S(2)}, u32[]{:S(2)}) %collective-permute-start.5) | collective-permute-done | bytes 2621472 | tf_op jit(solution)/shard_map/ppermute | solution.py:11
  361.3 5.7 maximum_select_fusion.4
  367.6 6.9 maximum_select_fusion.5
  375.0 13.3 %maximum_select_fusion = bf16[2,2048,1280]{2,1,0:T(8,128)(2,1)} fusion(bf16[2,1024,1280]{2,1,0:T(8,128)(2,1)} %maximum_select_fusion.3, bf16[2,1024,1280]{2,1,0:T(8,128)(2,1)} %collective-permute-done.2, pred[]{:T(512)S(6)} %eq.278), kind=kLoop, calls=%fused_computation.12 | loop fusion | flops 47185920 | bytes 20971520 | tf_op jit(solution)/shard_map/jit(_where)/select_n | solution.py:31
  388.3 8.7 %fusion.148 = (bf16[1,2048,1280]{2,1,0:T(8,128)(2,1)}, bf16[1,2048,1280]{2,1,0:T(8,128)(2,1)}) fusion(bf16[2,2048,1280]{2,1,0:T(8,128)(2,1)} %maximum_select_fusion), kind=kLoop, calls=%fused_computation.210 | loop fusion | bytes 20971520 | tf_op jit(solution)/shard_map/slice | solution.py:41
  397.0 8.0 %copy.71 = bf16[1,2048,1280]{1,2,0:T(8,128)(2,1)} copy(bf16[1,2048,1280]{2,1,0:T(8,128)(2,1)} %get-tuple-element.18) | data formatting | bytes 10485760 | tf_op jit(solution)/shard_map/slice | solution.py:41
  405.0 8.0 %copy.83 = bf16[1,2048,1280]{1,2,0:T(8,128)(2,1)} copy(bf16[1,2048,1280]{2,1,0:T(8,128)(2,1)} %get-tuple-element.19) | data formatting | bytes 10485760 | tf_op jit(solution)/shard_map/slice | solution.py:42
  413.0 15.4 %fusion.2 = (f32[16,256]{1,0:T(8,128)S(1)}, f32[16,2048,256]{2,1,0:T(8,128)}) fusion(pred[256,2048]{0,1:T(8,128)(4,1)S(1)} %iota_compare_fusion, bf16[2048,16,80]{0,2,1:T(8,128)(2,1)} %bitcast.111, bf16[256,16,80]{0,2,1:T(8,128)(2,1)S(1)} %bitcast.119), kind=kOutput, calls=%fused_computation.4 | convolution fusion | flops 1367339008 | bytes 39993344 | tf_op jit(solution)/shard_map/qhd,khd->hqk/dot_general | solution.py:43
  428.4 14.9 %fusion = f32[16,256]{1,0:T(8,128)} fusion(f32[16,2048,256]{2,1,0:T(8,128)} %get-tuple-element.39, f32[16,256]{1,0:T(8,128)S(1)} %get-tuple-element.38, pred[256,2048]{0,1:T(8,128)(4,1)S(1)} %iota_compare_fusion), kind=kLoop, calls=%fused_computation.2 | loop fusion | flops 33550336 | bytes 34111488 | tf_op jit(solution)/shard_map/reduce_sum | solution.py:50
  443.3 142.9 %collective-permute-done.6 = bf16[2,1024,1280]{2,1,0:T(8,128)(2,1)} collective-permute-done((bf16[2,1024,1280]{2,1,0:T(8,128)(2,1)}, bf16[2,1024,1280]{2,1,0:T(8,128)(2,1)}, u32[]{:S(2)}, u32[]{:S(2)}) %collective-permute-start.6) | collective-permute-done | bytes 5242912 | tf_op jit(solution)/shard_map/ppermute | solution.py:11
  586.2 13.2 %maximum_select_fusion.1 = bf16[2,2048,1280]{2,1,0:T(8,128)(2,1)} fusion(bf16[2,1024,1280]{2,1,0:T(8,128)(2,1)} %maximum_select_fusion.4, bf16[2,1024,1280]{2,1,0:T(8,128)(2,1)} %collective-permute-done.6, pred[]{:T(512)S(6)} %eq.287), kind=kLoop, calls=%fused_computation.13 | loop fusion | flops 47185920 | bytes 20971520 | tf_op jit(solution)/shard_map/jit(_where)/select_n | solution.py:31
  599.4 8.6 %fusion.149 = (bf16[1,2048,1280]{2,1,0:T(8,128)(2,1)}, bf16[1,2048,1280]{2,1,0:T(8,128)(2,1)}) fusion(bf16[2,2048,1280]{2,1,0:T(8,128)(2,1)} %maximum_select_fusion.1), kind=kLoop, calls=%fused_computation.211 | loop fusion | bytes 20971520 | tf_op jit(solution)/shard_map/slice | solution.py:41
  608.0 7.9 %copy.74 = bf16[1,2048,1280]{1,2,0:T(8,128)(2,1)} copy(bf16[1,2048,1280]{2,1,0:T(8,128)(2,1)} %get-tuple-element.20) | data formatting | bytes 10485760 | tf_op jit(solution)/shard_map/slice | solution.py:41
  615.9 8.1 %copy.86 = bf16[1,2048,1280]{1,2,0:T(8,128)(2,1)} copy(bf16[1,2048,1280]{2,1,0:T(8,128)(2,1)} %get-tuple-element.21) | data formatting | bytes 10485760 | tf_op jit(solution)/shard_map/slice | solution.py:42
  624.0 11.7 %fusion.6 = (f32[16,128]{1,0:T(8,128)S(1)}, f32[16,128,2048]{2,1,0:T(8,128)}) fusion(pred[128,2048]{1,0:T(8,128)(4,1)S(1)} %iota_compare_fusion.1, bf16[128,16,80]{0,2,1:T(8,128)(2,1)S(1)} %bitcast.124, bf16[2048,16,80]{0,2,1:T(8,128)(2,1)} %bitcast.109), kind=kOutput, calls=%fused_computation.9 | convolution fusion | flops 683669504 | bytes 22618112 | tf_op jit(solution)/shard_map/qhd,khd->hqk/dot_general | solution.py:43
  635.7 8.1 %fusion.9 = f32[16,80,128]{2,1,0:T(8,128)S(1)} fusion(bf16[2048,16,80]{0,2,1:T(8,128)(2,1)S(1)} %bitcast.117, f32[16,128,2048]{2,1,0:T(8,128)} %get-tuple-element.37, f32[16,128]{1,0:T(8,128)S(1)} %get-tuple-element.36, pred[128,2048]{1,0:T(8,128)(4,1)S(1)} %iota_compare_fusion.1), kind=kOutput, calls=%fused_computation.17 | convolution fusion | flops 687865856 | bytes 22945792 | tf_op jit(solution)/shard_map/hqk,khd->qhd/dot_general | solution.py:51
  644.2 8.1 %fusion.7 = f32[16,128]{1,0:T(8,128)S(1)} fusion(f32[16,128,2048]{2,1,0:T(8,128)} %get-tuple-element.37, f32[16,128]{1,0:T(8,128)S(1)} %get-tuple-element.36, pred[128,2048]{1,0:T(8,128)(4,1)S(1)} %iota_compare_fusion.1), kind=kLoop, calls=%fused_computation.10 | loop fusion | flops 16775168 | bytes 17055744 | tf_op jit(solution)/shard_map/reduce_sum | solution.py:50
  656.8 13.1 %maximum_select_fusion.2 = bf16[2,2048,1280]{2,1,0:T(8,128)(2,1)} fusion(bf16[2,1024,1280]{2,1,0:T(8,128)(2,1)} %maximum_select_fusion.5, bf16[2,1024,1280]{2,1,0:T(8,128)(2,1)} %collective-permute-done.11, pred[]{:T(512)S(6)} %eq.294), kind=kLoop, calls=%fused_computation.14 | loop fusion | flops 47185920 | bytes 20971520 | tf_op jit(solution)/shard_map/jit(_where)/select_n | solution.py:31
  669.9 8.6 %fusion.150 = (bf16[1,2048,1280]{2,1,0:T(8,128)(2,1)}, bf16[1,2048,1280]{2,1,0:T(8,128)(2,1)}) fusion(bf16[2,2048,1280]{2,1,0:T(8,128)(2,1)} %maximum_select_fusion.2), kind=kLoop, calls=%fused_computation.212 | loop fusion | bytes 20971520 | tf_op jit(solution)/shard_map/slice | solution.py:41
  678.5 8.2 %copy.78 = bf16[1,2048,1280]{1,2,0:T(8,128)(2,1)} copy(bf16[1,2048,1280]{2,1,0:T(8,128)(2,1)} %get-tuple-element.22) | data formatting | bytes 10485760 | tf_op jit(solution)/shard_map/slice | solution.py:41
  686.7 4.7 fusion.12
  697.9 7.9 %copy.90 = bf16[1,2048,1280]{1,2,0:T(8,128)(2,1)} copy(bf16[1,2048,1280]{2,1,0:T(8,128)(2,1)} %get-tuple-element.23) | data formatting | bytes 10485760 | tf_op jit(solution)/shard_map/slice | solution.py:42
  705.8 7.1 fusion.91
  715.9 17.7 %fusion.88 = f32[256,16,80]{0,2,1:T(8,128)} fusion(bf16[2048,16,80]{0,2,1:T(8,128)(2,1)} %bitcast.116, f32[16,2048,256]{2,1,0:T(8,128)} %get-tuple-element.39, f32[16,256]{1,0:T(8,128)S(1)} %get-tuple-element.38, pred[256,2048]{0,1:T(8,128)(4,1)S(1)} %iota_compare_fusion, f32[256,16]{0,1:T(8,128)S(1)} %get-tuple-element.17), kind=kOutput, calls=%fused_computation.115 | convolution fusion | flops 1376059392 | bytes 40665088 | tf_op jit(solution)/shard_map/hqk,khd->qhd/dot_general | solution.py:51
  735.2 5.4 convert_reduce_fusion
  740.7 33.0 %fusion.33 = bf16[256,2560]{1,0:T(8,128)(2,1)} fusion(bf16[5120,2560]{0,1:T(8,128)(2,1)} %all-gather.2.cloned.1.call-done, bf16[256,2560]{1,0:T(8,128)(2,1)S(1)} %get-tuple-element.40, bf16[2560,5120]{1,0:T(8,128)(2,1)} %param.14, f32[2560]{0:T(1024)S(1)} %copy-done.24, f32[256]{0:T(256)S(1)} %get-tuple-element.25, f32[256]{0:T(256)S(1)} %get-tuple-element.24), kind=kOutput, calls=%fused_computation.57 | convolution fusion | flops 13513523200 | bytes 55062528 | tf_op jit(solution)/shard_map/dot_general | solution.py:136
  (132 shorter events, 54.9 us)
Async XLA Ops:
  6.5 11.2 %copy-start.1 = (bf16[256,1280]{1,0:T(8,128)(2,1)S(1)}, bf16[256,1280]{1,0:T(8,128)(2,1)}, u32[]{:S(2)}) copy-start(bf16[256,1280]{1,0:T(8,128)(2,1)} %param.10) | copy-start | bytes 1966084
  6.5 11.2 %copy-start.2 = (bf16[256,1280]{1,0:T(8,128)(2,1)S(1)}, bf16[256,1280]{1,0:T(8,128)(2,1)}, u32[]{:S(2)}) copy-start(bf16[256,1280]{1,0:T(8,128)(2,1)} %param.11) | copy-start | bytes 1966084
  6.5 6.4 copy-start.3
  6.5 734.1 %all-gather.2.cloned.1.call-start = ((), (), s32[]{:S(2)}) async-start(), calls=%async_computation | async-start | bytes 27033600 | tf_op jit(solution)/shard_map/all_gather | solution.py:135
  9.7 8.0 %collective-permute-start = (bf16[2,256,1280]{2,1,0:T(8,128)(2,1)}, bf16[2,256,1280]{2,1,0:T(8,128)(2,1)}, u32[]{:S(2)}, u32[]{:S(2)}) collective-permute-start(bf16[2,256,1280]{2,1,0:T(8,128)(2,1)} %pad_maximum_fusion), channel_id=1, source_target_pairs={{0,1},{1,0},{2,3},{3,2},{4,5},{5,4},{6,7},{7,6},{8,9},{9,8},{10,11... | collective-permute-start | bytes 3932168 | tf_op jit(solution)/shard_map/ppermute | solution.py:11
  14.0 9.4 %copy-start.18 = (pred[4,1280]{1,0:T(4,128)(4,1)}, pred[4,1280]{1,0:T(4,128)(4,1)S(1)}, u32[]{:S(2)}) copy-start(pred[4,1280]{1,0:T(4,128)(4,1)S(1)} %iota_compare_fusion.3) | copy-start | bytes 15364
  17.7 5.6 copy-start.10
  21.1 109.5 %collective-permute-start.1 = (bf16[2,512,1280]{2,1,0:T(8,128)(2,1)}, bf16[2,512,1280]{2,1,0:T(8,128)(2,1)}, u32[]{:S(2)}, u32[]{:S(2)}) collective-permute-start(bf16[2,512,1280]{2,1,0:T(8,128)(2,1)} %maximum_select_fusion.6), channel_id=1, source_target_pairs={{0,2},{1,3},{2,0},{3,1},{4,6},{5,7},{6,4},{7,5},{8,10},{9,11},{10,... | collective-permute-start | bytes 7864328 | tf_op jit(solution)/shard_map/ppermute | solution.py:11
  23.4 8.0 %collective-permute-start.7 = (bf16[2,64,1280]{2,1,0:T(8,128)(2,1)}, bf16[2,64,1280]{2,1,0:T(8,128)(2,1)}, u32[]{:S(2)}, u32[]{:S(2)}) collective-permute-start(bf16[2,64,1280]{2,1,0:T(8,128)(2,1)} %pad_maximum_fusion.2), channel_id=1, source_target_pairs={{0,1},{1,0},{2,3},{3,2},{4,5},{5,4},{6,7},{7,6},{8,9},{9,8},{10,11... | collective-permute-start | bytes 983048 | tf_op jit(solution)/shard_map/ppermute | solution.py:11
  25.3 6.1 copy-start.16
  31.2 2.3 collective-permute-start.3
  32.8 93.6 %collective-permute-start.8 = (bf16[2,128,1280]{2,1,0:T(8,128)(2,1)S(1)}, bf16[2,128,1280]{2,1,0:T(8,128)(2,1)}, u32[]{:S(2)}, u32[]{:S(2)}) collective-permute-start(bf16[2,128,1280]{2,1,0:T(8,128)(2,1)S(1)} %maximum_select_fusion.11), channel_id=1, source_target_pairs={{0,2},{1,3},{2,0},{3,1},{4,6},{5,7},{6,4},{7,5},{8,10},{9,11},{10,... | collective-permute-start | bytes 1966088 | tf_op jit(solution)/shard_map/ppermute | solution.py:11
  33.9 148.4 %collective-permute-start.4 = (bf16[2,256,1280]{2,1,0:T(8,128)(2,1)S(1)}, bf16[2,256,1280]{2,1,0:T(8,128)(2,1)S(1)}, u32[]{:S(2)}, u32[]{:S(2)}) collective-permute-start(bf16[2,256,1280]{2,1,0:T(8,128)(2,1)S(1)} %maximum_select_fusion.9), channel_id=1, source_target_pairs={{0,2},{1,3},{2,0},{3,1},{4,6},{5,7},{6,4},{7,5},{8,10},{9,11},{10,... | collective-permute-start | bytes 3932168 | tf_op jit(solution)/shard_map/ppermute | solution.py:11
  129.1 60.0 %collective-permute-start.9 = (bf16[2,256,1280]{2,1,0:T(8,128)(2,1)}, bf16[2,256,1280]{2,1,0:T(8,128)(2,1)}, u32[]{:S(2)}, u32[]{:S(2)}) collective-permute-start(bf16[2,256,1280]{2,1,0:T(8,128)(2,1)} %maximum_select_fusion.10), channel_id=1, source_target_pairs={{0,4},{1,5},{2,6},{3,7},{4,0},{5,1},{6,2},{7,3},{8,12},{9,13},{10,... | collective-permute-start | bytes 3932168 | tf_op jit(solution)/shard_map/ppermute | solution.py:11
  137.8 237.2 %collective-permute-start.2 = (bf16[2,1024,1280]{2,1,0:T(8,128)(2,1)}, bf16[2,1024,1280]{2,1,0:T(8,128)(2,1)}, u32[]{:S(2)}, u32[]{:S(2)}) collective-permute-start(bf16[2,1024,1280]{2,1,0:T(8,128)(2,1)} %maximum_select_fusion.3), channel_id=1, source_target_pairs={{0,4},{1,5},{2,6},{3,7},{4,0},{5,1},{6,2},{7,3},{8,12},{9,13},{10,... | collective-permute-start | bytes 15728648 | tf_op jit(solution)/shard_map/ppermute | solution.py:11
  138.4 59.0 %copy-start.11 = (bf16[64,1280]{1,0:T(8,128)(2,1)S(1)}, bf16[64,1280]{1,0:T(8,128)(2,1)}, u32[]{:S(2)}) copy-start(bf16[64,1280]{1,0:T(8,128)(2,1)} %get-tuple-element.10) | copy-start | bytes 491524
  183.0 178.3 %collective-permute-start.5 = (bf16[2,512,1280]{2,1,0:T(8,128)(2,1)S(1)}, bf16[2,512,1280]{2,1,0:T(8,128)(2,1)}, u32[]{:S(2)}, u32[]{:S(2)}) collective-permute-start(bf16[2,512,1280]{2,1,0:T(8,128)(2,1)S(1)} %maximum_select_fusion.7), channel_id=1, source_target_pairs={{0,4},{1,5},{2,6},{3,7},{4,0},{5,1},{6,2},{7,3},{8,12},{9,13},{10,... | collective-permute-start | bytes 7864328 | tf_op jit(solution)/shard_map/ppermute | solution.py:11
  193.7 173.9 %collective-permute-start.10 = (bf16[2,512,1280]{2,1,0:T(8,128)(2,1)}, bf16[2,512,1280]{2,1,0:T(8,128)(2,1)}, u32[]{:S(2)}, u32[]{:S(2)}) collective-permute-start(bf16[2,512,1280]{2,1,0:T(8,128)(2,1)} %maximum_select_fusion.8), channel_id=1, source_target_pairs={{0,8},{1,9},{2,10},{3,11},{4,12},{5,13},{6,14},{7,15},{8,0},{9,1},... | collective-permute-start | bytes 7864328 | tf_op jit(solution)/shard_map/ppermute | solution.py:11
  367.0 219.2 %collective-permute-start.6 = (bf16[2,1024,1280]{2,1,0:T(8,128)(2,1)}, bf16[2,1024,1280]{2,1,0:T(8,128)(2,1)}, u32[]{:S(2)}, u32[]{:S(2)}) collective-permute-start(bf16[2,1024,1280]{2,1,0:T(8,128)(2,1)} %maximum_select_fusion.4), channel_id=1, source_target_pairs={{0,8},{1,9},{2,10},{3,11},{4,12},{5,13},{6,14},{7,15},{8,0},{9,1},... | collective-permute-start | bytes 15728648 | tf_op jit(solution)/shard_map/ppermute | solution.py:11
  374.5 282.4 %collective-permute-start.11 = (bf16[2,1024,1280]{2,1,0:T(8,128)(2,1)}, bf16[2,1024,1280]{2,1,0:T(8,128)(2,1)}, u32[]{:S(2)}, u32[]{:S(2)}) collective-permute-start(bf16[2,1024,1280]{2,1,0:T(8,128)(2,1)} %maximum_select_fusion.5), channel_id=1, source_target_pairs={{0,16},{1,17},{2,18},{3,19},{4,20},{5,21},{6,22},{7,23},{8,24},{9,... | collective-permute-start | bytes 15728648 | tf_op jit(solution)/shard_map/ppermute | solution.py:11
  405.0 8.0 %copy-start.7 = (bf16[256,1280]{0,1:T(8,128)(2,1)S(1)}, bf16[256,1280]{0,1:T(8,128)(2,1)}, u32[]{:S(2)}) copy-start(bf16[256,1280]{0,1:T(8,128)(2,1)} %copy.72) | copy-start | bytes 1966084
  615.9 8.1 %copy-start.8 = (bf16[128,1280]{0,1:T(8,128)(2,1)S(1)}, bf16[128,1280]{0,1:T(8,128)(2,1)}, u32[]{:S(2)}) copy-start(bf16[128,1280]{0,1:T(8,128)(2,1)} %copy.73) | copy-start | bytes 983044
  624.0 11.7 %copy-start.4 = (bf16[1,2048,1280]{1,2,0:T(8,128)(2,1)S(1)}, bf16[1,2048,1280]{1,2,0:T(8,128)(2,1)}, u32[]{:S(2)}) copy-start(bf16[1,2048,1280]{1,2,0:T(8,128)(2,1)} %copy.86) | copy-start | bytes 15728644
  644.1 8.2 %copy-start.23 = (pred[2,16]{1,0:T(4,128)(4,1)S(1)}, pred[2,16]{1,0:T(4,128)(4,1)}, u32[]{:S(2)}) copy-start(pred[2,16]{1,0:T(4,128)(4,1)} %get-tuple-element.33) | copy-start | bytes 100
  644.1 9.7 %copy-start.17 = (pred[2,1280]{1,0:T(4,128)(4,1)S(1)}, pred[2,1280]{1,0:T(4,128)(4,1)}, u32[]{:S(2)}) copy-start(pred[2,1280]{1,0:T(4,128)(4,1)} %copy-done.16) | copy-start | bytes 7684
  678.5 8.2 %copy-start.9 = (bf16[64,16,80]{2,1,0:T(8,128)(2,1)S(1)}, bf16[64,16,80]{2,1,0:T(8,128)(2,1)}, u32[]{:S(2)}) copy-start(bf16[64,16,80]{2,1,0:T(8,128)(2,1)} %reshape.373) | copy-start | bytes 491524
  691.4 3.2 copy-start
  691.4 5.6 copy-start.22
  705.8 7.8 copy-start.19
  715.8 17.7 %copy-start.5 = (f32[256,1280]{0,1:T(8,128)S(1)}, f32[256,1280]{0,1:T(8,128)}, u32[]{:S(2)}) copy-start(f32[256,1280]{0,1:T(8,128)} %copy.88) | copy-start | bytes 3932164
  715.9 17.7 %copy-start.6 = (f32[256,1280]{0,1:T(8,128)S(1)}, f32[256,1280]{0,1:T(8,128)}, u32[]{:S(2)}) copy-start(f32[256,1280]{0,1:T(8,128)} %copy.92) | copy-start | bytes 3932164
  735.2 5.5 copy-start.24
  (6 other events, 17.0 us)
Sparse Core Ops, SparseCore 0:
  10.2 235.2 all-gather.1
where the time goes:
time: 794 us; the launch traced here: 781 us
  waiting for transfers between devices  443 us (56%)
  other arithmetic  115 us (14%)
  matrix products  103 us (13%)
  local copies, waits for them, and re-layouts  96.2 us (12%)
  between operations  14.3 us (2%)
  starting transfers between devices  9.47 us (1%)
    ppermute x12, waiting for transfers between devices, swapped(): lax.ppermute(shard, axis, [(i, i ^ 1 << distance) for i in range(lax.axis...  442 us
    select_n x12, other arithmetic, join_halves(): jnp.where(upper, jnp.concatenate([other, mine], axis=-2), jnp.concatenate...  72.5 us
    slice x6, local copies, waits for them, and re-layouts, tier_attend(): key_heads = packed[0].reshape(key_count, head_count, HEAD_DIM)  49.9 us
    dot_general x1, matrix products, per_device(): terms = jnp.dot(hidden, down_whole, preferred_element_type=jnp.float32)  33 us
    dot_general x3, matrix products, tier_attend(): jnp.einsum('hqk,khd->qhd', shifted_exp.astype(jnp.bfloat16), value_heads,...  32.9 us
    dot_general x3, matrix products, tier_attend(): jnp.einsum('qhd,khd->hqk', query_heads, key_heads, preferred_element_type...  31.8 us
    reduce_sum x3, other arithmetic, tier_attend(): row_total = jnp.sum(shifted_exp, axis=-1)  25.3 us
    slice x3, local copies, waits for them, and re-layouts, tier_attend(): value_heads = packed[1].reshape(key_count, head_count, HEAD_DIM)  24 us
  transfers between devices with their start and end apart: 13, of which 5 were waited for; matrix products, arithmetic and copies ran while one was open for 36% of the time, Pallas kernels for 0%

commit v1 on v0

v1 whole, which is shorter than its diff:
```python
import functools
import math

import jax
import jax.numpy as jnp
from jax import lax
from jax.experimental import pallas as pl
from jax.experimental.pallas import tpu as pltpu
from jax.sharding import PartitionSpec as P

HEAD_DIM = 80
SEG0 = 2048
SLAB = 256
ONES_AT = 3 * HEAD_DIM
CHUNK = 128
MASKED = -1e30
VMEM_BYTES = 48 * 1024 * 1024


def reversed_bits(value, bits):
    return sum((value >> b & 1) << (bits - 1 - b) for b in range(bits))


def slot_level(slot, tiers):
    return tiers - 1 - slot.bit_length()


def pack_kernel(tiers, q_ref, k_ref, v_ref, out_ref):
    stride = 2 ** (tiers - 1)
    rows = q_ref.shape[0]
    per = rows // stride
    place = lax.broadcasted_iota(jnp.int32, (rows, rows), 0)
    source = lax.broadcasted_iota(jnp.int32, (rows, rows), 1)
    wanted = (place & (per - 1)) * stride + (place >> (per.bit_length() - 1))
    perm = (wanted == source).astype(jnp.bfloat16)
    sorted_rows = [
        jnp.dot(perm, ref[...], preferred_element_type=jnp.float32) for ref in (v_ref, k_ref, q_ref)
    ]
    ones = jnp.ones((rows, SLAB - ONES_AT), jnp.float32)
    for head in range(out_ref.shape[0]):
        cols = slice(head * HEAD_DIM, (head + 1) * HEAD_DIM)
        slab = jnp.concatenate([part[:, cols] for part in sorted_rows] + [ones], axis=1).astype(
            jnp.bfloat16
        )
        for slot in range(stride):
            res = reversed_bits(slot, tiers - 1) ^ head % stride
            out_ref[head, slot] = slab[res * per : (res + 1) * per]


def attend_kernel(tiers, heads_dev, group, info_ref, x_ref, *rest):
    extra_refs, (out_ref, acc, peak) = rest[: tiers - 1], rest[tiers - 1 :]
    stride = 2 ** (tiers - 1)
    span = x_ref.shape[2]
    seq_pos = info_ref[0]
    plane = seq_pos // group
    head_class = (seq_pos % group * heads_dev + pl.program_id(0)) % stride
    scale = HEAD_DIM ** (-0.5) * math.log2(math.e)

    sel_row = lax.broadcasted_iota(jnp.int32, (SLAB, SLAB), 0)
    sel_col = lax.broadcasted_iota(jnp.int32, (SLAB, SLAB), 1)
    to_keys = ((sel_row == sel_col + HEAD_DIM) & (sel_row >= 2 * HEAD_DIM) & (sel_row < ONES_AT)).astype(
        jnp.bfloat16
    )

    def queries(rows):
        return jnp.dot(rows, to_keys, preferred_element_type=jnp.float32).astype(jnp.bfloat16)

    def score(q, keys):
        return lax.dot_general(q, keys, (((1,), (1,)), ((), ())), preferred_element_type=jnp.float32)

    tile = stride * CHUNK
    row_ids = lax.broadcasted_iota(jnp.int32, (tile, 1), 0)
    row_slot = row_ids // CHUNK
    row_pos = row_ids % CHUNK
    row_res = jnp.zeros_like(row_ids)
    row_level = jnp.zeros_like(row_ids)
    for slot in range(stride):
        row_res = jnp.where(row_slot == slot, reversed_bits(slot, tiers - 1) ^ head_class, row_res)
        row_level = jnp.where(row_slot == slot, slot_level(slot, tiers), row_level)
    row_bias = []
    for level in range(tiers):
        count = jnp.minimum(row_level, level) + 1
        bias = jnp.zeros((tile, 1), jnp.float32)
        for times in range(2, tiers + 1):
            bias = jnp.where(count == times, math.log2(times), bias)
        row_bias.append(bias)
    key_pos = lax.broadcasted_iota(jnp.int32, (tile, CHUNK), 1)

    for chunk in range(span // CHUNK):
        lo, hi = chunk * CHUNK, (chunk + 1) * CHUNK
        q = queries(jnp.concatenate([x_ref[0, slot, lo:hi] for slot in range(stride)], axis=0))
        scores = []
        for slot in range(stride):
            key_res = reversed_bits(slot, tiers - 1) ^ head_class
            last = row_pos - (key_res > row_res).astype(jnp.int32)
            part = score(q, x_ref[0, slot, lo:hi])
            scores.append((slot, lo, hi, jnp.where(key_pos <= last, part, MASKED)))
            if lo:
                scores.append((slot, 0, lo, score(q, x_ref[0, slot, 0:lo])))
        top = functools.reduce(
            jnp.maximum, [jnp.max(part, axis=1, keepdims=True) for _, _, _, part in scores]
        )
        total = jnp.zeros((tile, SLAB), jnp.float32)
        for slot, start, stop, part in scores:
            shift = top * scale - row_bias[slot_level(slot, tiers)]
            weight = jnp.exp2(part * scale - shift).astype(jnp.bfloat16)
            total = total + jnp.dot(
                weight, x_ref[0, slot, start:stop], preferred_element_type=jnp.float32
            )
        for slot in range(stride):
            rows = slice(slot * CHUNK, (slot + 1) * CHUNK)
            acc[slot, lo:hi] = total[rows]
            peak[slot, lo:hi] = jnp.broadcast_to(top[rows], (CHUNK, peak.shape[2]))

    for tier in range(1, tiers):
        extra = extra_refs[tier - 1]

        @pl.when(plane // 2 ** (tier - 1) % 2 == 1)
        def _():
            for q_slot in range(stride // 2**tier):
                q = queries(x_ref[0, q_slot])
                parts = [score(q, extra[0, slot]) for slot in range(extra.shape[1])]
                old = peak[q_slot][:, :1]
                top = functools.reduce(
                    jnp.maximum, [jnp.max(part, axis=1, keepdims=True) for part in parts], old
                )
                total = acc[q_slot] * jnp.exp2((old - top) * scale)
                for slot, part in enumerate(parts):
                    times = min(slot_level(q_slot, tiers), slot_level(slot, tiers)) - tier + 1
                    shift = top * scale - math.log2(times)
                    weight = jnp.exp2(part * scale - shift).astype(jnp.bfloat16)
                    total = total + jnp.dot(weight, extra[0, slot], preferred_element_type=jnp.float32)
                acc[q_slot] = total
                peak[q_slot] = jnp.broadcast_to(top, (span, peak.shape[2]))

    width = out_ref.shape[3]
    for slot in range(stride):
        total = acc[slot]
        out_ref[0, slot] = (total[:, :width] / total[:, ONES_AT : ONES_AT + 1]).astype(jnp.bfloat16)


def attention(query_rows, key_rows, value_rows):
    rows, cols = query_rows.shape
    heads = cols // HEAD_DIM
    seq_count = lax.axis_size("seq")
    seq_pos = lax.axis_index("seq")
    total_rows = rows * seq_count
    tiers = 0
    while SEG0 * 2**tiers <= total_rows and total_rows % (SEG0 * 2**tiers) == 0:
        tiers += 1
    stride = 2 ** (tiers - 1)
    per = rows // stride
    group = SEG0 // rows
    heads_dev = heads // group
    span = SEG0 // stride

    packed = pl.pallas_call(
        functools.partial(pack_kernel, tiers),
        out_shape=jax.ShapeDtypeStruct((heads, stride, per, SLAB), jnp.bfloat16),
        in_specs=[pl.BlockSpec(memory_space=pltpu.VMEM)] * 3,
        out_specs=pl.BlockSpec(memory_space=pltpu.VMEM),
        compiler_params=pltpu.CompilerParams(vmem_limit_bytes=VMEM_BYTES),
        name="pack_heads",
    )(query_rows, key_rows, value_rows)

    groups = [[base + i for i in range(group)] for base in range(0, seq_count, group)]
    swapped = lax.all_to_all(
        packed.reshape(group, heads_dev, stride, per, SLAB), "seq", 0, 0, axis_index_groups=groups
    )
    local = swapped.transpose(1, 2, 0, 3, 4).reshape(heads_dev, stride, span, SLAB)

    extras = []
    block = local[:, : stride // 2, None, :, : 2 * HEAD_DIM]
    for tier in range(1, tiers):
        step = group * 2 ** (tier - 1)
        up = [(i, i + step) for i in range(seq_count) if i // step % 2 == 0]
        down = [(i + step, i) for i, _ in up]
        slots = stride // 2**tier
        flat = block.transpose(0, 1, 2, 4, 3)
        got = lax.ppermute(flat, "seq", up).transpose(0, 1, 2, 4, 3)
        keys = got.reshape(heads_dev, slots, -1, 2 * HEAD_DIM)
        filler = jnp.zeros(keys.shape[:3] + (HEAD_DIM,), jnp.bfloat16)
        ones = jnp.ones(keys.shape[:3] + (SLAB - ONES_AT,), jnp.bfloat16)
        extras.append(jnp.concatenate([keys, filler, ones], axis=-1))
        if tier + 1 < tiers:
            kept = slots // 2
            below = lax.ppermute(flat[:, :kept], "seq", down).transpose(0, 1, 2, 4, 3)
            upper = seq_pos // step % 2 == 1
            mine, other = block[:, :kept], jnp.where(upper, got[:, :kept], below)
            block = jnp.concatenate([mine, other], axis=2)

    out = pl.pallas_call(
        functools.partial(attend_kernel, tiers, heads_dev, group),
        grid=(heads_dev,),
        out_shape=jax.ShapeDtypeStruct((heads_dev, stride, span, 128), jnp.bfloat16),
        in_specs=[
            pl.BlockSpec(memory_space=pltpu.SMEM),
            pl.BlockSpec((1, stride, span, SLAB), lambda h: (h, 0, 0, 0)),
        ]
        + [pl.BlockSpec((1,) + extra.shape[1:], lambda h: (h, 0, 0, 0)) for extra in extras],
        out_specs=pl.BlockSpec((1, stride, span, 128), lambda h: (h, 0, 0, 0)),
        scratch_shapes=[
            pltpu.VMEM((stride, span, SLAB), jnp.float32),
            pltpu.VMEM((stride, span, 128), jnp.float32),
        ],
        compiler_params=pltpu.CompilerParams(vmem_limit_bytes=VMEM_BYTES),
        name="attend",
    )(seq_pos.reshape(1).astype(jnp.int32), local, *extras)

    back = out[..., :HEAD_DIM].reshape(heads_dev, stride, group, per, HEAD_DIM)
    back = back.transpose(2, 0, 1, 4, 3)
    home = lax.all_to_all(back, "seq", 0, 0, axis_index_groups=groups)
    home = home.reshape(heads, stride, HEAD_DIM, per)
    ordered = []
    for head in range(heads):
        order = [reversed_bits(res ^ head % stride, tiers - 1) for res in range(stride)]
        ordered.append(jnp.stack([home[head, slot] for slot in order]))
    whole = jnp.stack(ordered)
    return whole.transpose(3, 1, 0, 2).reshape(rows, cols)


def per_device(states, query_rows, key_rows, value_rows, out_proj, norm_gain, up_proj, down_proj):
    model_width = states.shape[1]
    mp_pos = lax.axis_index("mp")
    down_whole = lax.all_gather(down_proj, "seq", axis=1, tiled=True)
    attended = attention(query_rows, key_rows, value_rows)
    projected = jnp.dot(attended, out_proj, preferred_element_type=jnp.float32)
    share = lax.psum_scatter(projected, "mp", scatter_dimension=1, tiled=True)
    half_width = share.shape[1]
    states_share = lax.dynamic_slice_in_dim(states, mp_pos * half_width, half_width, 1)
    resid_share = (states_share.astype(jnp.float32) + share).astype(jnp.bfloat16)
    share_wide = resid_share.astype(jnp.float32)
    part_sum, part_squares = lax.psum(
        (
            jnp.sum(share_wide, axis=1, keepdims=True),
            jnp.sum(share_wide * share_wide, axis=1, keepdims=True),
        ),
        "mp",
    )
    row_mean = part_sum / model_width
    row_var = part_squares / model_width - row_mean * row_mean
    gain_share = lax.dynamic_slice_in_dim(norm_gain, mp_pos * half_width, half_width, 0)
    normed_share = (
        (share_wide - row_mean) * lax.rsqrt(row_var + 1e-05) * gain_share[None, :]
    ).astype(jnp.bfloat16)
    normed = lax.all_gather(normed_share, "mp", axis=1, tiled=True)
    hidden = jax.nn.gelu(
        jnp.dot(normed, up_proj, preferred_element_type=jnp.float32), approximate=False
    ).astype(jnp.bfloat16)
    terms = jnp.dot(hidden, down_whole, preferred_element_type=jnp.float32)
    ffn_part = lax.psum_scatter(
        terms.astype(jnp.bfloat16), "mp", scatter_dimension=1, tiled=True
    ).astype(jnp.float32)
    return (resid_share.astype(jnp.float32) + ffn_part).astype(jnp.bfloat16)


def solution(mesh):
    in_specs = (
        P("seq", None),
        P("seq", "mp"),
        P("seq", "mp"),
        P("seq", "mp"),
        P("mp", None),
        P(),
        P(None, "mp"),
        P("mp", "seq"),
    )
    out_specs = P("seq", "mp")
    return jax.shard_map(
        per_device, mesh=mesh, in_specs=in_specs, out_specs=out_specs, check_vma=False
    )
```

time: 794 us -> 278 us (0.35); the launches traced: 781 us -> 277 us
  waiting for transfers between devices: 443 us -> 102 us
  other arithmetic: 115 us -> 7.17 us
  local copies, waits for them, and re-layouts: 96.2 us -> 16.4 us
  matrix products: 103 us -> 43.4 us
  blocking collectives: 0 us -> 59.5 us
  Pallas kernels: 0 us -> 26 us
    ppermute x12 -> x3, waiting for transfers between devices: 442 us -> 101 us  [the longest x2 101 us: attention(): got = lax.ppermute(flat, 'seq', up).transpose(0, 1, 2, 4, 3)]
    select_n x20 -> x1, other arithmetic: 73.6 us -> 1.48 us  [attention(): mine, other = (block[:, :kept], jnp.where(upper, got[:, :kept], below))]
    slice x9 -> x2, local copies, waits for them, and re-layouts: 73.9 us -> 2.72 us  [the longest x1 1.87 us: attention(): mine, other = (block[:, :kept], jnp.where(upper, got[:, :kept], below))]
    dot_general x6 -> x0, matrix products: 64.7 us -> none  [the longest x3 32.9 us: tier_attend(): jnp.einsum('hqk,khd->qhd', shifted_exp.astype(jnp.bfloat16), value_heads,...]
    all_to_all x0 -> x2, blocking collectives: none -> 59.5 us  [the longest x1 36 us: attention(): lax.all_to_all(packed.reshape(group, heads_dev, stride, per, SLAB), 'seq'...]
    reduce_sum x5 -> x0, other arithmetic: 34.8 us -> none  [the longest x3 25.3 us: tier_attend(): row_total = jnp.sum(shifted_exp, axis=-1)]
    pallas_call x0 -> x2, Pallas kernels: none -> 26 us  [the longest x1 24.3 us: attention(): pl.pallas_call(functools.partial(attend_kernel, tiers, heads_dev, group),...]
  transfers between devices with their start and end apart: 13 -> 4, of which waited for: 5 -> 2; matrix products, arithmetic and copies ran while one was open for 36% -> 9% of each run, Pallas kernels for 0% -> 9%
where the time goes in v1:
time: 278 us; the launch traced here: 277 us
  waiting for transfers between devices  102 us (37%)
  blocking collectives  59.5 us (21%)
  matrix products  43.4 us (16%)
  Pallas kernels  26 us (9%)
  local copies, waits for them, and re-layouts  16.4 us (6%)
  between operations  13.6 us (5%)
  starting transfers between devices  8.94 us (3%)
  other arithmetic  7.17 us (3%)
    ppermute x2, waiting for transfers between devices, attention(): got = lax.ppermute(flat, 'seq', up).transpose(0, 1, 2, 4, 3)  101 us
    dot_general x1, matrix products, per_device(): terms = jnp.dot(hidden, down_whole, preferred_element_type=jnp.float32)  37.5 us
    all_to_all x1, blocking collectives, attention(): lax.all_to_all(packed.reshape(group, heads_dev, stride, per, SLAB), 'seq'...  36 us
    pallas_call x1, Pallas kernels, attention(): pl.pallas_call(functools.partial(attend_kernel, tiers, heads_dev, group),...  24.3 us
    all_to_all x1, blocking collectives, attention(): home = lax.all_to_all(back, 'seq', 0, 0, axis_index_groups=groups)  23.5 us
    ppermute x1, starting transfers between devices, attention(): below = lax.ppermute(flat[:, :kept], 'seq', down).transpose(0, 1, 2, 4, 3)  6.2 us
    dot_general x1, matrix products, per_device(): projected = jnp.dot(attended, out_proj, preferred_element_type=jnp.float32)  5.88 us
  transfers between devices with their start and end apart: 4, of which 2 were waited for; matrix products, arithmetic and copies ran while one was open for 9% of the time, Pallas kernels for 9%

profile of v1, /device:TPU:24, one launch (start us, length us, event | category | flops | bytes accessed | tf_op | source)
XLA Modules:
  0.0 277.1 jit_solution(17821692718367735012)
XLA Ops:
  6.5 0.7 all-gather.2.cloned.1.call-update
  7.3 1.1 copy-done
  8.3 1.1 copy-done.1
  9.4 1.1 copy-done.2
  10.5 1.7 pack_heads.1
  12.3 36.0 %all_to_all.10 = bf16[8,2,4,64,256]{4,3,2,1,0:T(8,128)(2,1)S(1)} all-to-all(bf16[8,2,4,64,256]{4,3,2,1,0:T(8,128)(2,1)S(1)} %bitcast.225), channel_id=1, replica_groups={{0,1,2,3,4,5,6,7},{8,9,10,11,12,13,14,15},{16,17,18,19,20,21,22,23},{24..., dimensions={0} | all-to-all | bytes 4194304 | tf_op jit(solution)/shard_map/all_to_all | solution.py:167
  48.2 0.1 copy.15
  48.4 1.1 slice_bitcast_fusion.1
  49.5 1.2 copy.16
  50.7 1.3 collective-permute-start
  52.0 0.9 slice.279
  52.8 6.2 %collective-permute-start.1 = (bf16[2,1,1,160,512]{3,4,1,0,2:T(8,128)(2,1)}, bf16[2,1,1,160,512]{3,4,1,0,2:T(8,128)(2,1)}, u32[]{:S(2)}, u32[]{:S(2)}) collective-permute-start(bf16[2,1,1,160,512]{3,4,1,0,2:T(8,128)(2,1)} %slice.279), channel_id=1, source_target_pairs={{8,0},{9,1},{10,2},{11,3},{12,4},{13,5},{14,6},{15,7},{24,16},{25,... | collective-permute-start | bytes 983048 | tf_op jit(solution)/shard_map/ppermute | solution.py:187
  59.0 1.9 slice.277
  60.9 38.7 %collective-permute-done = bf16[2,2,1,160,512]{4,3,2,1,0:T(8,128)(2,1)} collective-permute-done((bf16[2,2,1,160,512]{4,3,2,1,0:T(8,128)(2,1)}, bf16[2,2,1,160,512]{4,3,2,1,0:T(8,128)(2,1)}, u32[]{:S(2)}, u32[]{:S(2)}) %collective-permute-start) | collective-permute-done | bytes 655392 | tf_op jit(solution)/shard_map/ppermute | solution.py:180
  99.6 1.4 copy.17
  101.0 1.5 slice_select_fusion
  102.5 2.2 maximum_bitcast_fusion
  104.7 2.2 copy.18
  106.9 1.5 collective-permute-start.2
  108.3 0.1 pad.70.clone
  108.4 0.1 pad.71.clone
  108.5 1.5 maximum_maximum_fusion.rest_0_
  110.0 62.7 %collective-permute-done.2 = bf16[2,1,2,160,512]{4,3,2,1,0:T(8,128)(2,1)} collective-permute-done((bf16[2,1,2,160,512]{4,3,2,1,0:T(8,128)(2,1)}, bf16[2,1,2,160,512]{4,3,2,1,0:T(8,128)(2,1)}, u32[]{:S(2)}, u32[]{:S(2)}) %collective-permute-start.2) | collective-permute-done | bytes 655392 | tf_op jit(solution)/shard_map/ppermute | solution.py:180
  172.7 2.2 copy.19
  174.9 1.5 maximum_maximum_fusion.1.rest_1_
  176.4 24.3 %attend.1 = bf16[2,4,512,128]{3,2,1,0:T(8,128)(2,1)S(1)} custom-call(s32[1]{0:T(128)} %bitcast.info_ref, bf16[2,4,512,256]{3,2,1,0:T(8,128)(2,1)S(1)} %bitcast.224, bf16[2,2,512,256]{3,2,1,0:T(8,128)(2,1)S(1)} %maximum_maximum_fusion.rest_0_, bf16[2,1,1024,256]{3,2,1,0:T(8,128)(2,1)S(1)} %maximum_maximum_fusion.1.rest_1_), custom_call_target="tpu_custom_call" | custom-call | tf_op jit(solution)/shard_map/attend/pallas_call | solution.py:192
  200.7 0.1 copy.23
  200.8 23.5 %all_to_all.11 = bf16[8,2,4,80,64]{3,4,2,1,0:T(8,128)(2,1)S(1)} all-to-all(bf16[8,2,4,80,64]{3,4,2,1,0:T(8,128)(2,1)S(1)} %bitcast.234), channel_id=1, replica_groups={{0,1,2,3,4,5,6,7},{8,9,10,11,12,13,14,15},{16,17,18,19,20,21,22,23},{24..., dimensions={0} | all-to-all | bytes 1310720 | tf_op jit(solution)/shard_map/all_to_all | solution.py:212
  225.0 0.7 copy.21
  225.7 1.2 reshape.50
  226.9 5.9 %convert_reduce_fusion = (f32[256]{0:T(256)S(1)}, f32[256]{0:T(256)S(1)}, bf16[256,2560]{1,0:T(8,128)(2,1)}) fusion(bf16[256,1280]{1,0:T(8,128)(2,1)S(1)} %reshape.50, bf16[1280,2560]{1,0:T(8,128)(2,1)} %param.12, bf16[256,2560]{1,0:T(8,128)(2,1)S(1)} %copy-done.4), kind=kOutput, calls=%fused_computation.22 | convolution fusion | flops 1682308608 | bytes 9832448 | tf_op jit(solution)/shard_map/dot_general | solution.py:227
  232.8 37.5 %fusion.12 = bf16[256,2560]{1,0:T(8,128)(2,1)} fusion(bf16[5120,2560]{0,1:T(8,128)(2,1)} %all-gather.2.cloned.1.call-done, bf16[256,2560]{1,0:T(8,128)(2,1)} %get-tuple-element.75, bf16[2560,5120]{1,0:T(8,128)(2,1)} %param.14, f32[2560]{0:T(1024)S(1)} %copy-done.5, f32[256]{0:T(256)S(1)} %get-tuple-element.74, f32[256]{0:T(256)S(1)} %get-tuple-element.73), kind=kOutput, calls=%fused_computation.27 | convolution fusion | flops 13513523200 | bytes 55062528 | tf_op jit(solution)/shard_map/dot_general | solution.py:250
  (35 shorter events, 0.6 us)
Async XLA Ops:
  6.5 226.2 %all-gather.2.cloned.1.call-start = ((), (), s32[]{:S(2)}) async-start(), calls=%async_computation.2 | async-start | bytes 27033600 | tf_op jit(solution)/shard_map/all_gather | solution.py:225
  7.3 1.1 copy-start
  8.3 1.1 copy-start.1
  9.4 1.1 copy-start.2
  50.7 48.9 %collective-permute-start = (bf16[2,2,1,160,512]{4,3,2,1,0:T(8,128)(2,1)}, bf16[2,2,1,160,512]{4,3,2,1,0:T(8,128)(2,1)}, u32[]{:S(2)}, u32[]{:S(2)}) collective-permute-start(bf16[2,2,1,160,512]{4,3,2,1,0:T(8,128)(2,1)} %copy.16), channel_id=1, source_target_pairs={{0,8},{1,9},{2,10},{3,11},{4,12},{5,13},{6,14},{7,15},{16,24},{17,... | collective-permute-start | bytes 1966088 | tf_op jit(solution)/shard_map/ppermute | solution.py:180
  52.8 48.2 %collective-permute-start.1 = (bf16[2,1,1,160,512]{3,4,1,0,2:T(8,128)(2,1)}, bf16[2,1,1,160,512]{3,4,1,0,2:T(8,128)(2,1)}, u32[]{:S(2)}, u32[]{:S(2)}) collective-permute-start(bf16[2,1,1,160,512]{3,4,1,0,2:T(8,128)(2,1)} %slice.279), channel_id=1, source_target_pairs={{8,0},{9,1},{10,2},{11,3},{12,4},{13,5},{14,6},{15,7},{24,16},{25,... | collective-permute-start | bytes 983048 | tf_op jit(solution)/shard_map/ppermute | solution.py:187
  101.0 7.5 %copy-start.3 = (bf16[2,2,1,160,512]{3,4,1,0,2:T(8,128)(2,1)}, bf16[2,2,1,160,512]{3,4,1,0,2:T(8,128)(2,1)S(1)}, u32[]{:S(2)}) copy-start(bf16[2,2,1,160,512]{3,4,1,0,2:T(8,128)(2,1)S(1)} %copy.17) | copy-start | bytes 1966084
  106.9 65.8 %collective-permute-start.2 = (bf16[2,1,2,160,512]{4,3,2,1,0:T(8,128)(2,1)}, bf16[2,1,2,160,512]{4,3,2,1,0:T(8,128)(2,1)}, u32[]{:S(2)}, u32[]{:S(2)}) collective-permute-start(bf16[2,1,2,160,512]{4,3,2,1,0:T(8,128)(2,1)} %copy.18), channel_id=1, source_target_pairs={{0,16},{1,17},{2,18},{3,19},{4,20},{5,21},{6,22},{7,23},{8,24},{9,... | collective-permute-start | bytes 1966088 | tf_op jit(solution)/shard_map/ppermute | solution.py:180
  200.8 26.0 %copy-start.4 = (bf16[256,2560]{1,0:T(8,128)(2,1)S(1)}, bf16[256,2560]{1,0:T(8,128)(2,1)}, u32[]{:S(2)}) copy-start(bf16[256,2560]{1,0:T(8,128)(2,1)} %param.8) | copy-start | bytes 3932164
  226.9 5.9 %copy-start.5 = (f32[2560]{0:T(1024)S(1)}, f32[2560]{0:T(1024)}, u32[]{:S(2)}) copy-start(f32[2560]{0:T(1024)} %param.13) | copy-start | bytes 30724
Sparse Core Ops, SparseCore 0:
  10.2 195.5 all-gather.1

commit v2 on v1

--- a/solution.py
+++ b/solution.py
@@ -219,11 +219,86 @@
     return whole.transpose(3, 1, 0, 2).reshape(rows, cols)
 
 
+def lift_kernel(att_ref, states_ref, proj_ref, gain_ref, up_ref, resid_ref, hidden_ref, normed):
+    @pl.when(pl.program_id(0) == 0)
+    def _():
+        projected = jnp.dot(att_ref[...], proj_ref[...], preferred_element_type=jnp.float32)
+        resid = (states_ref[...].astype(jnp.float32) + projected).astype(jnp.bfloat16)
+        resid_ref[...] = resid
+        wide = resid.astype(jnp.float32)
+        centered = wide - jnp.mean(wide, axis=1, keepdims=True)
+        var = jnp.mean(centered * centered, axis=1, keepdims=True)
+        normed[...] = (centered * lax.rsqrt(var + 1e-05) * gain_ref[...]).astype(jnp.bfloat16)
+
+    raw = jnp.dot(normed[...], up_ref[...], preferred_element_type=jnp.float32)
+    hidden_ref[...] = (0.5 * raw * (1.0 + lax.erf(raw * math.sqrt(0.5)))).astype(jnp.bfloat16)
+
+
+def lower_kernel(hidden_ref, down_ref, resid_ref, out_ref):
+    mixed = lax.dot_general(
+        hidden_ref[...],
+        down_ref[...],
+        (((1,), (1,)), ((), ())),
+        preferred_element_type=jnp.float32,
+    )
+    out_ref[...] = (resid_ref[...].astype(jnp.float32) + mixed).astype(jnp.bfloat16)
+
+
+def feed_forward(attended, states, out_proj, norm_gain, up_proj, down_rows):
+    rows, width = states.shape
+    units = up_proj.shape[1]
+    step = math.gcd(units, 512)
+    whole = lambda i: (0, 0)
+    resid, hidden = pl.pallas_call(
+        lift_kernel,
+        grid=(units // step,),
+        out_shape=(
+            jax.ShapeDtypeStruct((rows, width), jnp.bfloat16),
+            jax.ShapeDtypeStruct((rows, units), jnp.bfloat16),
+        ),
+        in_specs=[
+            pl.BlockSpec(attended.shape, whole),
+            pl.BlockSpec((rows, width), whole),
+            pl.BlockSpec(out_proj.shape, whole),
+            pl.BlockSpec((1, width), whole),
+            pl.BlockSpec((width, step), lambda i: (0, i)),
+        ],
+        out_specs=(
+            pl.BlockSpec((rows, width), whole),
+            pl.BlockSpec((rows, step), lambda i: (0, i)),
+        ),
+        scratch_shapes=[pltpu.VMEM((rows, width), jnp.bfloat16)],
+        compiler_params=pltpu.CompilerParams(vmem_limit_bytes=VMEM_BYTES),
+        cost_estimate=pl.CostEstimate(
+            flops=2 * rows * width * (units + attended.shape[1]),
+            bytes_accessed=2 * width * (units + attended.shape[1]),
+            transcendentals=rows * units,
+        ),
+        name="project_and_lift",
+    )(attended, states, out_proj, norm_gain.reshape(1, width), up_proj)
+    part = math.gcd(width, 256)
+    return pl.pallas_call(
+        lower_kernel,
+        grid=(width // part,),
+        out_shape=jax.ShapeDtypeStruct((rows, width), jnp.bfloat16),
+        in_specs=[
+            pl.BlockSpec((rows, units), whole),
+            pl.BlockSpec((part, units), lambda i: (i, 0)),
+            pl.BlockSpec((rows, part), lambda i: (0, i)),
+        ],
+        out_specs=pl.BlockSpec((rows, part), lambda i: (0, i)),
+        compiler_params=pltpu.CompilerParams(vmem_limit_bytes=VMEM_BYTES),
+        name="lower",
+    )(hidden, down_rows, resid)
+
+
 def per_device(states, query_rows, key_rows, value_rows, out_proj, norm_gain, up_proj, down_proj):
     model_width = states.shape[1]
     mp_pos = lax.axis_index("mp")
-    down_whole = lax.all_gather(down_proj, "seq", axis=1, tiled=True)
+    down_rows = lax.all_gather(down_proj.T, "seq", axis=0, tiled=True)
     attended = attention(query_rows, key_rows, value_rows)
+    if lax.axis_size("mp") == 1:
+        return feed_forward(attended, states, out_proj, norm_gain, up_proj, down_rows)
     projected = jnp.dot(attended, out_proj, preferred_element_type=jnp.float32)
     share = lax.psum_scatter(projected, "mp", scatter_dimension=1, tiled=True)
     half_width = share.shape[1]
@@ -247,7 +322,9 @@
     hidden = jax.nn.gelu(
         jnp.dot(normed, up_proj, preferred_element_type=jnp.float32), approximate=False
     ).astype(jnp.bfloat16)
-    terms = jnp.dot(hidden, down_whole, preferred_element_type=jnp.float32)
+    terms = lax.dot_general(
+        hidden, down_rows, (((1,), (1,)), ((), ())), preferred_element_type=jnp.float32
+    )
     ffn_part = lax.psum_scatter(
         terms.astype(jnp.bfloat16), "mp", scatter_dimension=1, tiled=True
     ).astype(jnp.float32)

time: 278 us -> 274 us (0.986)
  matrix products: 43.4 us -> 0 us
  Pallas kernels: 26 us -> 60.8 us
  blocking collectives: 59.5 us -> 36 us
  waiting for transfers between devices: 102 us -> 117 us
  starting transfers between devices: 8.94 us -> 17.2 us
  local copies, waits for them, and re-layouts: 16.4 us -> 21.1 us
    dot_general x2 -> x0, matrix products: 43.4 us -> none  [the longest x1 37.5 us: per_device(): terms = jnp.dot(hidden, down_whole, preferred_element_type=jnp.float32)]
    pallas_call x0 -> x2, Pallas kernels: none -> 34.8 us  [the longest x1 19.3 us: feed_forward(): pl.pallas_call(lift_kernel, grid=(units // step,), out_shape=(jax.ShapeDt...]
    all_to_all x1 -> x0, blocking collectives: 23.5 us -> none  [attention(): home = lax.all_to_all(back, 'seq', 0, 0, axis_index_groups=groups)]
    all_to_all x0 -> x1, waiting for transfers between devices: none -> 15.4 us  [attention(): home = lax.all_to_all(back, 'seq', 0, 0, axis_index_groups=groups)]
    all_to_all x0 -> x1, starting transfers between devices: none -> 8.28 us  [attention(): home = lax.all_to_all(back, 'seq', 0, 0, axis_index_groups=groups)]
    unnamed x12 -> x16, local copies, waits for them, and re-layouts: 3.27 us -> 6.95 us
  transfers between devices with their start and end apart: 4 -> 5, of which waited for: 2 -> 3; matrix products, arithmetic and copies ran while one was open for 9% -> 8% of each run, Pallas kernels for 9% -> 17%
where the time goes in v2:
time: 274 us; the launch traced here: 273 us
  waiting for transfers between devices  117 us (43%)
  Pallas kernels  60.8 us (22%)
  blocking collectives  36 us (13%)
  local copies, waits for them, and re-layouts  21.1 us (8%)
  starting transfers between devices  17.2 us (6%)
  between operations  13.6 us (5%)
  other arithmetic  7.19 us (3%)
    ppermute x2, waiting for transfers between devices, attention(): got = lax.ppermute(flat, 'seq', up).transpose(0, 1, 2, 4, 3)  101 us
    all_to_all x1, blocking collectives, attention(): lax.all_to_all(packed.reshape(group, heads_dev, stride, per, SLAB), 'seq'...  36 us
    pallas_call x1, Pallas kernels, attention(): pl.pallas_call(functools.partial(attend_kernel, tiers, heads_dev, group),...  24.3 us
    pallas_call x1, Pallas kernels, feed_forward(): pl.pallas_call(lift_kernel, grid=(units // step,), out_shape=(jax.ShapeDt...  19.3 us
    pallas_call x1, Pallas kernels, feed_forward(): pl.pallas_call(lower_kernel, grid=(width // part,), out_shape=jax.ShapeDt...  15.5 us
    all_to_all x1, waiting for transfers between devices, attention(): home = lax.all_to_all(back, 'seq', 0, 0, axis_index_groups=groups)  15.4 us
    all_to_all x1, starting transfers between devices, attention(): home = lax.all_to_all(back, 'seq', 0, 0, axis_index_groups=groups)  8.28 us
    unnamed x16, local copies, waits for them, and re-layouts  6.95 us
  transfers between devices with their start and end apart: 5, of which 3 were waited for; matrix products, arithmetic and copies ran while one was open for 8% of the time, Pallas kernels for 17%

profile of v2, /device:TPU:24, one launch (start us, length us, event | category | flops | bytes accessed | tf_op | source)
XLA Modules:
  0.0 273.3 jit_solution(5004635317849707846)
XLA Ops:
  6.5 0.7 all-gather.2.cloned.1.call-update
  7.3 1.1 copy-done.3
  8.3 1.1 copy-done.4
  9.4 1.1 copy-done.5
  10.5 1.7 pack_heads.1
  12.3 36.0 %all_to_all.10 = bf16[8,2,4,64,256]{4,3,2,1,0:T(8,128)(2,1)S(1)} all-to-all(bf16[8,2,4,64,256]{4,3,2,1,0:T(8,128)(2,1)S(1)} %bitcast.222), channel_id=1, replica_groups={{0,1,2,3,4,5,6,7},{8,9,10,11,12,13,14,15},{16,17,18,19,20,21,22,23},{24..., dimensions={0} | all-to-all | bytes 4194304 | tf_op jit(solution)/shard_map/all_to_all | solution.py:167
  48.4 1.1 slice_bitcast_fusion.1
  49.5 1.2 copy.35
  50.7 1.3 collective-permute-start
  52.0 0.8 slice.279
  52.8 6.2 %collective-permute-start.1 = (bf16[2,1,1,160,512]{3,4,1,0,2:T(8,128)(2,1)}, bf16[2,1,1,160,512]{3,4,1,0,2:T(8,128)(2,1)}, u32[]{:S(2)}, u32[]{:S(2)}) collective-permute-start(bf16[2,1,1,160,512]{3,4,1,0,2:T(8,128)(2,1)} %slice.279), channel_id=1, source_target_pairs={{8,0},{9,1},{10,2},{11,3},{12,4},{13,5},{14,6},{15,7},{24,16},{25,... | collective-permute-start | bytes 983048 | tf_op jit(solution)/shard_map/ppermute | solution.py:187
  59.0 1.9 slice.277
  60.8 38.7 %collective-permute-done = bf16[2,2,1,160,512]{4,3,2,1,0:T(8,128)(2,1)} collective-permute-done((bf16[2,2,1,160,512]{4,3,2,1,0:T(8,128)(2,1)}, bf16[2,2,1,160,512]{4,3,2,1,0:T(8,128)(2,1)}, u32[]{:S(2)}, u32[]{:S(2)}) %collective-permute-start) | collective-permute-done | bytes 655392 | tf_op jit(solution)/shard_map/ppermute | solution.py:180
  99.6 1.4 copy.36
  101.0 1.5 slice_select_fusion
  102.5 2.2 maximum_bitcast_fusion
  104.7 2.2 copy.37
  106.9 1.5 collective-permute-start.2
  108.5 1.5 maximum_maximum_fusion.rest_0_
  110.0 62.6 %collective-permute-done.2 = bf16[2,1,2,160,512]{4,3,2,1,0:T(8,128)(2,1)} collective-permute-done((bf16[2,1,2,160,512]{4,3,2,1,0:T(8,128)(2,1)}, bf16[2,1,2,160,512]{4,3,2,1,0:T(8,128)(2,1)}, u32[]{:S(2)}, u32[]{:S(2)}) %collective-permute-start.2) | collective-permute-done | bytes 655392 | tf_op jit(solution)/shard_map/ppermute | solution.py:180
  172.7 2.2 copy.38
  174.9 1.5 maximum_maximum_fusion.1.rest_1_
  176.4 24.3 %attend.1 = bf16[2,4,512,128]{3,2,1,0:T(8,128)(2,1)S(1)} custom-call(s32[1]{0:T(128)} %bitcast.info_ref, bf16[2,4,512,256]{3,2,1,0:T(8,128)(2,1)S(1)} %bitcast.221, bf16[2,2,512,256]{3,2,1,0:T(8,128)(2,1)S(1)} %maximum_maximum_fusion.rest_0_, bf16[2,1,1024,256]{3,2,1,0:T(8,128)(2,1)S(1)} %maximum_maximum_fusion.1.rest_1_), custom_call_target="tpu_custom_call" | custom-call | tf_op jit(solution)/shard_map/attend/pallas_call | solution.py:192
  200.7 1.1 copy.42
  201.8 8.3 %all-to-all-start.1 = ((bf16[8,2,4,80,64]{3,4,2,1,0:T(8,128)(2,1)}), bf16[8,2,4,80,64]{3,4,2,1,0:T(8,128)(2,1)S(1)}, u32[]{:S(2)}, u32[]{:S(2)}) async-start(bf16[8,2,4,80,64]{3,4,2,1,0:T(8,128)(2,1)} %bitcast.218), calls=%async_computation.1 | async-start | bytes 2097152 | tf_op jit(solution)/shard_map/all_to_all | solution.py:212
  210.1 15.4 %all-to-all-done.1 = bf16[8,2,4,80,64]{3,4,2,1,0:T(8,128)(2,1)S(1)} async-done(((bf16[8,2,4,80,64]{3,4,2,1,0:T(8,128)(2,1)}), bf16[8,2,4,80,64]{3,4,2,1,0:T(8,128)(2,1)S(1)}, u32[]{:S(2)}, u32[]{:S(2)}) %all-to-all-start.1) | async-done | bytes 655392 | tf_op jit(solution)/shard_map/all_to_all | solution.py:212
  226.8 1.2 reshape.34.att_ref
  228.0 1.3 copy-done
  229.3 19.3 %project_and_lift.1 = (bf16[256,2560]{1,0:T(8,128)(2,1)S(1)}, bf16[256,5120]{1,0:T(8,128)(2,1)S(1)}) custom-call(bf16[256,1280]{1,0:T(8,128)(2,1)S(1)} %reshape.34.att_ref, bf16[256,2560]{1,0:T(8,128)(2,1)S(1)} %copy-done, bf16[1280,2560]{1,0:T(8,128)(2,1)} %proj_ref.1, f32[1,2560]{1,0:T(1,128)S(1)} %reshape.35.gain_ref, bf16[2560,5120]{1,0:T(8,128)(2,1)} %up_ref.1), custom_call_target="tpu_custom_call" | custom-call | flops 8388608000 | bytes 32768000 | tf_op jit(solution)/shard_map/project_and_lift/pallas_call | solution.py:252
  248.6 1.0 copy-done.1
  249.6 1.3 copy-done.2
  251.0 15.5 %lower.1 = bf16[256,2560]{1,0:T(8,128)(2,1)} custom-call(bf16[256,5120]{1,0:T(8,128)(2,1)S(1)} %get-tuple-element.7.hidden_ref, bf16[2560,5120]{1,0:T(8,128)(2,1)} %all-gather.2.cloned.1.call-done.down_ref, bf16[256,2560]{1,0:T(8,128)(2,1)S(1)} %copy-done.2), custom_call_target="tpu_custom_call" | custom-call | tf_op jit(solution)/shard_map/lower/pallas_call | solution.py:280
  (40 shorter events, 1.5 us)
Async XLA Ops:
  6.5 243.1 %all-gather.2.cloned.1.call-start = ((), (), s32[]{:S(2)}) async-start(), calls=%async_computation.2 | async-start | bytes 27033600 | tf_op jit(solution)/shard_map/all_gather | solution.py:298
  7.3 1.1 copy-start.3
  8.3 1.1 copy-start.4
  9.4 1.1 copy-start.5
  50.7 48.9 %collective-permute-start = (bf16[2,2,1,160,512]{4,3,2,1,0:T(8,128)(2,1)}, bf16[2,2,1,160,512]{4,3,2,1,0:T(8,128)(2,1)}, u32[]{:S(2)}, u32[]{:S(2)}) collective-permute-start(bf16[2,2,1,160,512]{4,3,2,1,0:T(8,128)(2,1)} %copy.35), channel_id=1, source_target_pairs={{0,8},{1,9},{2,10},{3,11},{4,12},{5,13},{6,14},{7,15},{16,24},{17,... | collective-permute-start | bytes 1966088 | tf_op jit(solution)/shard_map/ppermute | solution.py:180
  52.8 48.2 %collective-permute-start.1 = (bf16[2,1,1,160,512]{3,4,1,0,2:T(8,128)(2,1)}, bf16[2,1,1,160,512]{3,4,1,0,2:T(8,128)(2,1)}, u32[]{:S(2)}, u32[]{:S(2)}) collective-permute-start(bf16[2,1,1,160,512]{3,4,1,0,2:T(8,128)(2,1)} %slice.279), channel_id=1, source_target_pairs={{8,0},{9,1},{10,2},{11,3},{12,4},{13,5},{14,6},{15,7},{24,16},{25,... | collective-permute-start | bytes 983048 | tf_op jit(solution)/shard_map/ppermute | solution.py:187
  101.0 5.9 %copy-start.6 = (bf16[2,2,1,160,512]{3,4,1,0,2:T(8,128)(2,1)}, bf16[2,2,1,160,512]{3,4,1,0,2:T(8,128)(2,1)S(1)}, u32[]{:S(2)}) copy-start(bf16[2,2,1,160,512]{3,4,1,0,2:T(8,128)(2,1)S(1)} %copy.36) | copy-start | bytes 1966084
  106.9 65.8 %collective-permute-start.2 = (bf16[2,1,2,160,512]{4,3,2,1,0:T(8,128)(2,1)}, bf16[2,1,2,160,512]{4,3,2,1,0:T(8,128)(2,1)}, u32[]{:S(2)}, u32[]{:S(2)}) collective-permute-start(bf16[2,1,2,160,512]{4,3,2,1,0:T(8,128)(2,1)} %copy.37), channel_id=1, source_target_pairs={{0,16},{1,17},{2,18},{3,19},{4,20},{5,21},{6,22},{7,23},{8,24},{9,... | collective-permute-start | bytes 1966088 | tf_op jit(solution)/shard_map/ppermute | solution.py:180
  200.7 9.4 %copy-start.7 = (f32[2560]{0:T(1024)S(1)}, f32[2560]{0:T(1024)}, u32[]{:S(2)}) copy-start(f32[2560]{0:T(1024)} %param.13) | copy-start | bytes 30724
  201.8 23.7 %all-to-all-start.1 = ((bf16[8,2,4,80,64]{3,4,2,1,0:T(8,128)(2,1)}), bf16[8,2,4,80,64]{3,4,2,1,0:T(8,128)(2,1)S(1)}, u32[]{:S(2)}, u32[]{:S(2)}) async-start(bf16[8,2,4,80,64]{3,4,2,1,0:T(8,128)(2,1)} %bitcast.218), calls=%async_computation.1 | async-start | bytes 2097152 | tf_op jit(solution)/shard_map/all_to_all | solution.py:212
  228.0 1.3 copy-start
  248.6 1.1 copy-start.1
  249.6 1.3 copy-start.2
Sparse Core Ops, SparseCore 0:
  10.2 195.5 all-gather.1

commit v3 on v2

--- a/solution.py
+++ b/solution.py
@@ -47,23 +47,21 @@
             out_ref[head, slot] = slab[res * per : (res + 1) * per]
 
 
-def attend_kernel(tiers, heads_dev, group, info_ref, x_ref, *rest):
-    extra_refs, (out_ref, acc, peak) = rest[: tiers - 1], rest[tiers - 1 :]
-    stride = 2 ** (tiers - 1)
-    span = x_ref.shape[2]
-    seq_pos = info_ref[0]
-    plane = seq_pos // group
-    head_class = (seq_pos % group * heads_dev + pl.program_id(0)) % stride
-    scale = HEAD_DIM ** (-0.5) * math.log2(math.e)
-
+def query_part(rows):
     sel_row = lax.broadcasted_iota(jnp.int32, (SLAB, SLAB), 0)
     sel_col = lax.broadcasted_iota(jnp.int32, (SLAB, SLAB), 1)
     to_keys = ((sel_row == sel_col + HEAD_DIM) & (sel_row >= 2 * HEAD_DIM) & (sel_row < ONES_AT)).astype(
         jnp.bfloat16
     )
-
-    def queries(rows):
-        return jnp.dot(rows, to_keys, preferred_element_type=jnp.float32).astype(jnp.bfloat16)
+    return jnp.dot(rows, to_keys, preferred_element_type=jnp.float32).astype(jnp.bfloat16)
+
+
+def segment_kernel(tiers, heads_dev, group, info_ref, x_ref, out_ref, acc_ref, peak_ref):
+    stride = 2 ** (tiers - 1)
+    span = x_ref.shape[2]
+    seq_pos = info_ref[0]
+    head_class = (seq_pos % group * heads_dev + pl.program_id(0)) % stride
+    scale = HEAD_DIM ** (-0.5) * math.log2(math.e)
 
     def score(q, keys):
         return lax.dot_general(q, keys, (((1,), (1,)), ((), ())), preferred_element_type=jnp.float32)
@@ -88,7 +86,7 @@
 
     for chunk in range(span // CHUNK):
         lo, hi = chunk * CHUNK, (chunk + 1) * CHUNK
-        q = queries(jnp.concatenate([x_ref[0, slot, lo:hi] for slot in range(stride)], axis=0))
+        q = query_part(jnp.concatenate([x_ref[0, slot, lo:hi] for slot in range(stride)], axis=0))
         scores = []
         for slot in range(stride):
             key_res = reversed_bits(slot, tiers - 1) ^ head_class
@@ -107,36 +105,67 @@
             total = total + jnp.dot(
                 weight, x_ref[0, slot, start:stop], preferred_element_type=jnp.float32
             )
+        width = out_ref.shape[3]
         for slot in range(stride):
             rows = slice(slot * CHUNK, (slot + 1) * CHUNK)
-            acc[slot, lo:hi] = total[rows]
-            peak[slot, lo:hi] = jnp.broadcast_to(top[rows], (CHUNK, peak.shape[2]))
-
+            if slot < stride // 2:
+                acc_ref[0, slot, lo:hi] = total[rows]
+                peak_ref[0, slot, lo:hi] = jnp.broadcast_to(top[rows], (CHUNK, peak_ref.shape[3]))
+            else:
+                done = total[rows, :width] / total[rows, ONES_AT : ONES_AT + 1]
+                out_ref[0, slot - stride // 2, lo:hi] = done.astype(jnp.bfloat16)
+
+
+def earlier_kernel(tiers, group, info_ref, x_ref, acc_in, peak_in, *rest):
+    extra_refs, (out_ref, acc, peak) = rest[:-3], rest[-3:]
+    half, span = x_ref.shape[1:3]
+    stride = 2 * half
+    plane = info_ref[0] // group
+    scale = HEAD_DIM ** (-0.5) * math.log2(math.e)
+    depth = 2 * HEAD_DIM
+    acc[...] = acc_in[0]
+    peak[...] = peak_in[0]
+    at = 0
     for tier in range(1, tiers):
-        extra = extra_refs[tier - 1]
+        extras = extra_refs[at : at + 2 ** (tier - 1)]
+        at += 2 ** (tier - 1)
 
         @pl.when(plane // 2 ** (tier - 1) % 2 == 1)
         def _():
             for q_slot in range(stride // 2**tier):
-                q = queries(x_ref[0, q_slot])
-                parts = [score(q, extra[0, slot]) for slot in range(extra.shape[1])]
+                q = query_part(x_ref[0, q_slot])[:, :depth]
+                parts = [
+                    (slot, ref, jnp.dot(q, ref[0, slot], preferred_element_type=jnp.float32))
+                    for ref in extras
+                    for slot in range(ref.shape[1])
+                ]
                 old = peak[q_slot][:, :1]
                 top = functools.reduce(
-                    jnp.maximum, [jnp.max(part, axis=1, keepdims=True) for part in parts], old
+                    jnp.maximum, [jnp.max(part, axis=1, keepdims=True) for _, _, part in parts], old
                 )
-                total = acc[q_slot] * jnp.exp2((old - top) * scale)
-                for slot, part in enumerate(parts):
+                keep = jnp.exp2((old - top) * scale)
+                numer = acc[q_slot, :, :128] * keep
+                denom = acc[q_slot, :, ONES_AT : ONES_AT + 1] * keep
+                for slot, ref, part in parts:
                     times = min(slot_level(q_slot, tiers), slot_level(slot, tiers)) - tier + 1
-                    shift = top * scale - math.log2(times)
-                    weight = jnp.exp2(part * scale - shift).astype(jnp.bfloat16)
-                    total = total + jnp.dot(weight, extra[0, slot], preferred_element_type=jnp.float32)
-                acc[q_slot] = total
+                    weight = jnp.exp2(part * scale - (top * scale - math.log2(times)))
+                    denom = denom + jnp.sum(weight, axis=1, keepdims=True)
+                    numer = (
+                        numer
+                        + lax.dot_general(
+                            weight.astype(jnp.bfloat16),
+                            ref[0, slot],
+                            (((1,), (1,)), ((), ())),
+                            preferred_element_type=jnp.float32,
+                        )[:, :128]
+                    )
+                acc[q_slot, :, :128] = numer
+                acc[q_slot, :, 128:] = jnp.broadcast_to(denom, (span, SLAB - 128))
                 peak[q_slot] = jnp.broadcast_to(top, (span, peak.shape[2]))
 
-    width = out_ref.shape[3]
-    for slot in range(stride):
-        total = acc[slot]
-        out_ref[0, slot] = (total[:, :width] / total[:, ONES_AT : ONES_AT + 1]).astype(jnp.bfloat16)
+    for slot in range(half):
+        done = acc[slot, :, :128] / acc[slot, :, ONES_AT : ONES_AT + 1]
+        out_ref[0, slot] = done.astype(jnp.bfloat16)
 
 
 def attention(query_rows, key_rows, value_rows):
@@ -169,48 +198,72 @@
     )
     local = swapped.transpose(1, 2, 0, 3, 4).reshape(heads_dev, stride, span, SLAB)
 
+    half = stride // 2
+    flat = local[:, :half, :, : 2 * HEAD_DIM].transpose(0, 1, 3, 2)
     extras = []
-    block = local[:, : stride // 2, None, :, : 2 * HEAD_DIM]
     for tier in range(1, tiers):
-        step = group * 2 ** (tier - 1)
-        up = [(i, i + step) for i in range(seq_count) if i // step % 2 == 0]
-        down = [(i + step, i) for i, _ in up]
-        slots = stride // 2**tier
-        flat = block.transpose(0, 1, 2, 4, 3)
-        got = lax.ppermute(flat, "seq", up).transpose(0, 1, 2, 4, 3)
-        keys = got.reshape(heads_dev, slots, -1, 2 * HEAD_DIM)
-        filler = jnp.zeros(keys.shape[:3] + (HEAD_DIM,), jnp.bfloat16)
-        ones = jnp.ones(keys.shape[:3] + (SLAB - ONES_AT,), jnp.bfloat16)
-        extras.append(jnp.concatenate([keys, filler, ones], axis=-1))
-        if tier + 1 < tiers:
-            kept = slots // 2
-            below = lax.ppermute(flat[:, :kept], "seq", down).transpose(0, 1, 2, 4, 3)
-            upper = seq_pos // step % 2 == 1
-            mine, other = block[:, :kept], jnp.where(upper, got[:, :kept], below)
-            block = jnp.concatenate([mine, other], axis=2)
-
-    out = pl.pallas_call(
-        functools.partial(attend_kernel, tiers, heads_dev, group),
+        bit = 2 ** (tier - 1)
+        for twist in range(bit):
+            pairs = [
+                (i, ((i // group | bit) ^ twist) * group + i % group)
+                for i in range(seq_count)
+                if i // group & bit == 0
+            ]
+            extras.append(lax.ppermute(flat[:, : stride // 2**tier], "seq", pairs))
+
+    info = seq_pos.reshape(1).astype(jnp.int32)
+    smem = pl.BlockSpec(memory_space=pltpu.SMEM)
+
+    def per_head(shape):
+        return pl.BlockSpec((1,) + tuple(shape[1:]), lambda h: (h,) + (0,) * (len(shape) - 1))
+
+    upper_shape = (heads_dev, stride - half, span, 128)
+    acc_shape = (heads_dev, half, span, SLAB)
+    peak_shape = (heads_dev, half, span, 128)
+    upper, acc, peak = pl.pallas_call(
+        functools.partial(segment_kernel, tiers, heads_dev, group),
         grid=(heads_dev,),
-        out_shape=jax.ShapeDtypeStruct((heads_dev, stride, span, 128), jnp.bfloat16),
-        in_specs=[
-            pl.BlockSpec(memory_space=pltpu.SMEM),
-            pl.BlockSpec((1, stride, span, SLAB), lambda h: (h, 0, 0, 0)),
-        ]
-        + [pl.BlockSpec((1,) + extra.shape[1:], lambda h: (h, 0, 0, 0)) for extra in extras],
-        out_specs=pl.BlockSpec((1, stride, span, 128), lambda h: (h, 0, 0, 0)),
+        out_shape=(
+            jax.ShapeDtypeStruct(upper_shape, jnp.bfloat16),
+            jax.ShapeDtypeStruct(acc_shape, jnp.float32),
+            jax.ShapeDtypeStruct(peak_shape, jnp.float32),
+        ),
+        in_specs=[smem, per_head(local.shape)],
+        out_specs=(per_head(upper_shape), per_head(acc_shape), per_head(peak_shape)),
+        compiler_params=pltpu.CompilerParams(vmem_limit_bytes=VMEM_BYTES),
+        cost_estimate=pl.CostEstimate(
+            flops=heads_dev * SEG0 * SEG0 * 4 * SLAB,
+            bytes_accessed=heads_dev * SEG0 * SLAB * 6,
+            transcendentals=heads_dev * SEG0 * SEG0,
+        ),
+        name="segment_attend",
+    )(info, local)
+
+    groups = [[base + i for i in range(group)] for base in range(0, seq_count, group)]
+
+    def send_home(part):
+        part = part[..., :HEAD_DIM].reshape(heads_dev, -1, group, per, HEAD_DIM)
+        part = part.transpose(2, 0, 1, 4, 3)
+        part = lax.all_to_all(part, "seq", 0, 0, axis_index_groups=groups)
+        return part.reshape(heads, -1, HEAD_DIM, per)
+
+    upper_home = send_home(upper)
+    lower = pl.pallas_call(
+        functools.partial(earlier_kernel, tiers, group),
+        grid=(heads_dev,),
+        out_shape=jax.ShapeDtypeStruct(peak_shape, jnp.bfloat16),
+        in_specs=[smem, pl.BlockSpec((1, half, span, SLAB), lambda h: (h, 0, 0, 0))]
+        + [per_head(acc_shape), per_head(peak_shape)]
+        + [per_head(extra.shape) for extra in extras],
+        out_specs=per_head(peak_shape),
         scratch_shapes=[
-            pltpu.VMEM((stride, span, SLAB), jnp.float32),
-            pltpu.VMEM((stride, span, 128), jnp.float32),
+            pltpu.VMEM((half, span, SLAB), jnp.float32),
+            pltpu.VMEM((half, span, 128), jnp.float32),
         ],
         compiler_params=pltpu.CompilerParams(vmem_limit_bytes=VMEM_BYTES),
-        name="attend",
-    )(seq_pos.reshape(1).astype(jnp.int32), local, *extras)
-
-    back = out[..., :HEAD_DIM].reshape(heads_dev, stride, group, per, HEAD_DIM)
-    back = back.transpose(2, 0, 1, 4, 3)
-    home = lax.all_to_all(back, "seq", 0, 0, axis_index_groups=groups)
-    home = home.reshape(heads, stride, HEAD_DIM, per)
+        name="earlier_segments",
+    )(info, local, acc, peak, *extras)
+    home = jnp.concatenate([send_home(lower), upper_home], axis=1)
     ordered = []
     for head in range(heads):
         order = [reversed_bits(res ^ head % stride, tiers - 1) for res in range(stride)]

time: 274 us -> 242 us (0.88); the launches traced: 273 us -> 237 us
  blocking collectives: 36 us -> 0 us
  Pallas kernels: 60.8 us -> 68.3 us
  other arithmetic: 7.19 us -> 0.44 us
  waiting for transfers between devices: 117 us -> 120 us
    ppermute x3, waiting for transfers between devices: 101 us -> 38.9 us  [attention(): extras.append(lax.ppermute(flat[:, :stride // 2 ** tier], 'seq', pairs))]
    all_to_all x1 -> x0, blocking collectives: 36 us -> none  [attention(): lax.all_to_all(packed.reshape(group, heads_dev, stride, per, SLAB), 'seq'...]
    all_gather x1, waiting for transfers between devices: 0.01 us -> 34.3 us  [per_device(): down_rows = lax.all_gather(down_proj.T, 'seq', axis=0, tiled=True)]
    all_to_all x1 -> x3, waiting for transfers between devices: 15.4 us -> 46.3 us  [the longest x1 32.5 us: attention(): lax.all_to_all(packed.reshape(group, heads_dev, stride, per, SLAB), 'seq'...]
    pallas_call x1 -> x2, Pallas kernels: 24.3 us -> 30.3 us  [the longest x1 15.2 us: attention(): pl.pallas_call(functools.partial(earlier_kernel, tiers, group), grid=(hea...]
    transpose x4 -> x0, local copies, waits for them, and re-layouts: 5.68 us -> none  [the longest x2 3.36 us: attention(): flat = block.transpose(0, 1, 2, 4, 3)]
    ppermute x3, starting transfers between devices: 8.93 us -> 3.86 us  [attention(): extras.append(lax.ppermute(flat[:, :stride // 2 ** tier], 'seq', pairs))]
    all_to_all x1 -> x3, starting transfers between devices: 8.28 us -> 12.2 us  [the longest x2 7.84 us: send_home(): part = lax.all_to_all(part, 'seq', 0, 0, axis_index_groups=groups)]
  transfers between devices with their start and end apart: 5 -> 7, of which waited for: 3 -> 5; matrix products, arithmetic and copies ran while one was open for 8% -> 5% of each run, Pallas kernels for 17% -> 22%
where the time goes in v3:
time: 242 us; the launch traced here: 237 us
  waiting for transfers between devices  120 us (50%)
  Pallas kernels  68.3 us (28%)
  local copies, waits for them, and re-layouts  18.6 us (8%)
  starting transfers between devices  16.1 us (7%)
  between operations  13.6 us (6%)
    ppermute x3, waiting for transfers between devices, attention(): extras.append(lax.ppermute(flat[:, :stride // 2 ** tier], 'seq', pairs))  38.9 us
    all_gather x1, waiting for transfers between devices, per_device(): down_rows = lax.all_gather(down_proj.T, 'seq', axis=0, tiled=True)  34.3 us
    all_to_all x1, waiting for transfers between devices, attention(): lax.all_to_all(packed.reshape(group, heads_dev, stride, per, SLAB), 'seq'...  32.5 us
    pallas_call x1, Pallas kernels, feed_forward(): pl.pallas_call(lift_kernel, grid=(units // step,), out_shape=(jax.ShapeDt...  19.3 us
    pallas_call x1, Pallas kernels, feed_forward(): pl.pallas_call(lower_kernel, grid=(width // part,), out_shape=jax.ShapeDt...  15.5 us
    pallas_call x1, Pallas kernels, attention(): pl.pallas_call(functools.partial(earlier_kernel, tiers, group), grid=(hea...  15.2 us
    pallas_call x1, Pallas kernels, attention(): pl.pallas_call(functools.partial(segment_kernel, tiers, heads_dev, group)...  15.1 us
    all_to_all x2, waiting for transfers between devices, send_home(): part = lax.all_to_all(part, 'seq', 0, 0, axis_index_groups=groups)  13.8 us
  transfers between devices with their start and end apart: 7, of which 5 were waited for; matrix products, arithmetic and copies ran while one was open for 5% of the time, Pallas kernels for 22%

profile of v3, /device:TPU:24, one launch (start us, length us, event | category | flops | bytes accessed | tf_op | source)
XLA Modules:
  0.0 237.2 jit_solution(1688294088119326585)
XLA Ops:
  6.5 0.7 all-gather.2.cloned.1.call-update
  7.3 1.1 copy-done.4
  8.3 1.1 copy-done.5
  9.4 1.1 copy-done.6
  10.5 3.2 %pack_heads.1 = bf16[16,4,64,256]{3,2,1,0:T(8,128)(2,1)} custom-call(bf16[256,1280]{1,0:T(8,128)(2,1)S(1)} %copy-done.4, bf16[256,1280]{1,0:T(8,128)(2,1)S(1)} %copy-done.5, bf16[256,1280]{1,0:T(8,128)(2,1)S(1)} %copy-done.6), custom_call_target="tpu_custom_call" | custom-call | tf_op jit(solution)/shard_map/pack_heads/pallas_call | solution.py:186
  13.7 4.3 %all-to-all-start = ((bf16[8,2,4,64,256]{4,3,2,1,0:T(8,128)(2,1)}), bf16[8,2,4,64,256]{4,3,2,1,0:T(8,128)(2,1)}, u32[]{:S(2)}, u32[]{:S(2)}) async-start(bf16[8,2,4,64,256]{4,3,2,1,0:T(8,128)(2,1)} %bitcast.1), calls=%async_computation | async-start | bytes 4194304 | tf_op jit(solution)/shard_map/all_to_all | solution.py:196
  18.0 32.5 %all-to-all-done = bf16[8,2,4,64,256]{4,3,2,1,0:T(8,128)(2,1)} async-done(((bf16[8,2,4,64,256]{4,3,2,1,0:T(8,128)(2,1)}), bf16[8,2,4,64,256]{4,3,2,1,0:T(8,128)(2,1)}, u32[]{:S(2)}, u32[]{:S(2)}) %all-to-all-start) | async-done | bytes 2097184 | tf_op jit(solution)/shard_map/all_to_all | solution.py:196
  50.5 1.8 copy.37
  52.4 1.2 copy.42
  53.6 1.7 slice.274
  55.3 1.3 collective-permute-start.1
  56.6 1.3 collective-permute-start.2
  57.9 1.3 collective-permute-start
  59.2 15.1 %segment_attend.1 = (bf16[2,2,512,128]{3,2,1,0:T(8,128)(2,1)S(1)}, f32[2,2,512,256]{3,2,1,0:T(8,128)S(1)}, f32[2,2,512,128]{3,2,1,0:T(8,128)S(1)}) custom-call(s32[1]{0:T(128)} %bitcast.info_ref, bf16[2,4,512,256]{3,2,1,0:T(8,128)(2,1)S(1)} %bitcast.215), custom_call_target="tpu_custom_call" | custom-call | flops 8589934592 | bytes 6291456 | tf_op jit(solution)/shard_map/segment_attend/pallas_call | solution.py:223
  74.3 1.3 copy-done
  75.6 0.9 copy.45
  76.5 4.3 %all-to-all-start.2 = ((bf16[8,2,2,80,64]{3,4,2,1,0:T(8,128)(2,1)}), bf16[8,2,2,80,64]{3,4,2,1,0:T(8,128)(2,1)}, u32[]{:S(2)}, u32[]{:S(2)}) async-start(bf16[8,2,2,80,64]{3,4,2,1,0:T(8,128)(2,1)} %bitcast.221), calls=%async_computation.2 | async-start | bytes 1048576 | tf_op jit(solution)/shard_map/all_to_all | solution.py:247
  80.9 13.8 %collective-permute-done.1.rest_1_ = bf16[2,1,160,512]{3,2,1,0:T(8,128)(2,1)S(1)} collective-permute-done((bf16[2,1,160,512]{3,2,1,0:T(8,128)(2,1)}, bf16[2,1,160,512]{3,2,1,0:T(8,128)(2,1)S(1)}, u32[]{:S(2)}, u32[]{:S(2)}) %collective-permute-start.1) | collective-permute-done | bytes 327712 | tf_op jit(solution)/shard_map/ppermute | solution.py:212
  94.7 25.1 %collective-permute-done.rest_0_ = bf16[2,2,160,512]{3,2,1,0:T(8,128)(2,1)} collective-permute-done((bf16[2,2,160,512]{3,2,1,0:T(8,128)(2,1)}, bf16[2,2,160,512]{3,2,1,0:T(8,128)(2,1)}, u32[]{:S(2)}, u32[]{:S(2)}) %collective-permute-start) | collective-permute-done | bytes 655392 | tf_op jit(solution)/shard_map/ppermute | solution.py:212
  119.8 15.2 %earlier_segments.1 = bf16[2,2,512,128]{3,2,1,0:T(8,128)(2,1)S(1)} custom-call(s32[1]{0:T(128)} %bitcast.info_ref, bf16[2,4,512,256]{3,2,1,0:T(8,128)(2,1)S(1)} %bitcast.216, f32[2,2,512,256]{3,2,1,0:T(8,128)} %copy-done, f32[2,2,512,128]{3,2,1,0:T(8,128)S(1)} %get-tuple-element.11.peak_in, bf16[2,2,160,512]{3,2,1,0:T(8,128)(2,1)} %collective-permute-done.rest_0_, ...), custom_call_target="tpu_custom_call" | custom-call | tf_op jit(solution)/shard_map/earlier_segments/pallas_call | solution.py:251
  135.0 0.8 copy.46
  135.9 3.5 %all-to-all-start.1 = ((bf16[8,2,2,80,64]{3,4,2,1,0:T(8,128)(2,1)}), bf16[8,2,2,80,64]{3,4,2,1,0:T(8,128)(2,1)S(1)}, u32[]{:S(2)}, u32[]{:S(2)}) async-start(bf16[8,2,2,80,64]{3,4,2,1,0:T(8,128)(2,1)} %bitcast.211), calls=%async_computation.1 | async-start | bytes 1048576 | tf_op jit(solution)/shard_map/all_to_all | solution.py:247
  139.4 0.9 slice_bitcast_fusion.38
  140.3 0.9 slice_bitcast_fusion.3
  141.2 13.8 %all-to-all-done.1 = bf16[8,2,2,80,64]{3,4,2,1,0:T(8,128)(2,1)S(1)} async-done(((bf16[8,2,2,80,64]{3,4,2,1,0:T(8,128)(2,1)}), bf16[8,2,2,80,64]{3,4,2,1,0:T(8,128)(2,1)S(1)}, u32[]{:S(2)}, u32[]{:S(2)}) %all-to-all-start.1) | async-done | bytes 327712 | tf_op jit(solution)/shard_map/all_to_all | solution.py:247
  156.3 1.2 reshape.34.att_ref
  157.5 1.3 copy-done.1
  158.8 19.3 %project_and_lift.1 = (bf16[256,2560]{1,0:T(8,128)(2,1)S(1)}, bf16[256,5120]{1,0:T(8,128)(2,1)S(1)}) custom-call(bf16[256,1280]{1,0:T(8,128)(2,1)S(1)} %reshape.34.att_ref, bf16[256,2560]{1,0:T(8,128)(2,1)S(1)} %copy-done.1, bf16[1280,2560]{1,0:T(8,128)(2,1)} %proj_ref.1, f32[1,2560]{1,0:T(1,128)S(1)} %reshape.35.gain_ref, bf16[2560,5120]{1,0:T(8,128)(2,1)} %up_ref.1), custom_call_target="tpu_custom_call" | custom-call | flops 8388608000 | bytes 32768000 | tf_op jit(solution)/shard_map/project_and_lift/pallas_call | solution.py:305
  178.2 1.0 copy-done.2
  179.2 34.3 %all-gather.2.cloned.1.call-done.down_ref = bf16[2560,5120]{1,0:T(8,128)(2,1)} async-done(((bf16[80,5120]{1,0:T(8,128)(2,1)}), bf16[2560,5120]{1,0:T(8,128)(2,1)}) %all-gather.2.cloned.1.call-update) | async-done | bytes 26214416 | tf_op jit(solution)/shard_map/all_gather | solution.py:351
  213.5 1.3 copy-done.3
  214.8 15.5 %lower.1 = bf16[256,2560]{1,0:T(8,128)(2,1)} custom-call(bf16[256,5120]{1,0:T(8,128)(2,1)S(1)} %get-tuple-element.13.hidden_ref, bf16[2560,5120]{1,0:T(8,128)(2,1)} %all-gather.2.cloned.1.call-done.down_ref, bf16[256,2560]{1,0:T(8,128)(2,1)S(1)} %copy-done.3), custom_call_target="tpu_custom_call" | custom-call | tf_op jit(solution)/shard_map/lower/pallas_call | solution.py:333
  (33 shorter events, 1.3 us)
Async XLA Ops:
  6.5 206.9 %all-gather.2.cloned.1.call-start = ((), (), s32[]{:S(2)}) async-start(), calls=%async_computation.3 | async-start | bytes 27033600 | tf_op jit(solution)/shard_map/all_gather | solution.py:351
  7.3 1.1 copy-start.4
  8.3 1.1 copy-start.5
  9.4 1.1 copy-start.6
  13.7 36.8 %all-to-all-start = ((bf16[8,2,4,64,256]{4,3,2,1,0:T(8,128)(2,1)}), bf16[8,2,4,64,256]{4,3,2,1,0:T(8,128)(2,1)}, u32[]{:S(2)}, u32[]{:S(2)}) async-start(bf16[8,2,4,64,256]{4,3,2,1,0:T(8,128)(2,1)} %bitcast.1), calls=%async_computation | async-start | bytes 4194304 | tf_op jit(solution)/shard_map/all_to_all | solution.py:196
  55.3 39.3 %collective-permute-start.1 = (bf16[2,1,160,512]{3,2,1,0:T(8,128)(2,1)}, bf16[2,1,160,512]{3,2,1,0:T(8,128)(2,1)S(1)}, u32[]{:S(2)}, u32[]{:S(2)}) collective-permute-start(bf16[2,1,160,512]{3,2,1,0:T(8,128)(2,1)} %slice.274), channel_id=1, source_target_pairs={{0,16},{1,17},{2,18},{3,19},{4,20},{5,21},{6,22},{7,23},{8,24},{9,... | collective-permute-start | bytes 983048 | tf_op jit(solution)/shard_map/ppermute | solution.py:212
  56.6 38.0 %collective-permute-start.2 = (bf16[2,1,160,512]{3,2,1,0:T(8,128)(2,1)}, bf16[2,1,160,512]{3,2,1,0:T(8,128)(2,1)}, u32[]{:S(2)}, u32[]{:S(2)}) collective-permute-start(bf16[2,1,160,512]{3,2,1,0:T(8,128)(2,1)} %slice.274), channel_id=1, source_target_pairs={{0,24},{1,25},{2,26},{3,27},{4,28},{5,29},{6,30},{7,31},{8,16},{9,... | collective-permute-start | bytes 983048 | tf_op jit(solution)/shard_map/ppermute | solution.py:212
  57.9 61.8 %collective-permute-start = (bf16[2,2,160,512]{3,2,1,0:T(8,128)(2,1)}, bf16[2,2,160,512]{3,2,1,0:T(8,128)(2,1)}, u32[]{:S(2)}, u32[]{:S(2)}) collective-permute-start(bf16[2,2,160,512]{3,2,1,0:T(8,128)(2,1)} %bitcast.223), channel_id=1, source_target_pairs={{0,8},{1,9},{2,10},{3,11},{4,12},{5,13},{6,14},{7,15},{16,24},{17,... | collective-permute-start | bytes 1966088 | tf_op jit(solution)/shard_map/ppermute | solution.py:212
  74.3 1.3 copy-start
  75.6 5.2 %copy-start.7 = (f32[2560]{0:T(1024)S(1)}, f32[2560]{0:T(1024)}, u32[]{:S(2)}) copy-start(f32[2560]{0:T(1024)} %param.13) | copy-start | bytes 30724
  76.5 59.3 %all-to-all-start.2 = ((bf16[8,2,2,80,64]{3,4,2,1,0:T(8,128)(2,1)}), bf16[8,2,2,80,64]{3,4,2,1,0:T(8,128)(2,1)}, u32[]{:S(2)}, u32[]{:S(2)}) async-start(bf16[8,2,2,80,64]{3,4,2,1,0:T(8,128)(2,1)} %bitcast.221), calls=%async_computation.2 | async-start | bytes 1048576 | tf_op jit(solution)/shard_map/all_to_all | solution.py:247
  135.9 19.2 %all-to-all-start.1 = ((bf16[8,2,2,80,64]{3,4,2,1,0:T(8,128)(2,1)}), bf16[8,2,2,80,64]{3,4,2,1,0:T(8,128)(2,1)S(1)}, u32[]{:S(2)}, u32[]{:S(2)}) async-start(bf16[8,2,2,80,64]{3,4,2,1,0:T(8,128)(2,1)} %bitcast.211), calls=%async_computation.1 | async-start | bytes 1048576 | tf_op jit(solution)/shard_map/all_to_all | solution.py:247
  157.5 1.3 copy-start.1
  178.1 1.1 copy-start.2
  213.5 1.3 copy-start.3
Sparse Core Ops, SparseCore 0:
  10.2 203.2 all-gather.1

commit v4 on v3

--- a/solution.py
+++ b/solution.py
@@ -14,7 +14,7 @@
 ONES_AT = 3 * HEAD_DIM
 CHUNK = 128
 MASKED = -1e30
-VMEM_BYTES = 48 * 1024 * 1024
+VMEM_BYTES = 30 * 1024 * 1024
 
 
 def reversed_bits(value, bits):
@@ -287,21 +287,36 @@
     hidden_ref[...] = (0.5 * raw * (1.0 + lax.erf(raw * math.sqrt(0.5)))).astype(jnp.bfloat16)
 
 
-def lower_kernel(hidden_ref, down_ref, resid_ref, out_ref):
-    mixed = lax.dot_general(
-        hidden_ref[...],
-        down_ref[...],
-        (((1,), (1,)), ((), ())),
-        preferred_element_type=jnp.float32,
+def lower_kernel(info_ref, hidden_ref, mine_ref, other_ref, resid_ref, out_ref):
+    hidden = hidden_ref[...]
+
+    def product(ref):
+        count, cols, depth = ref.shape
+        return lax.dot_general(
+            hidden,
+            ref[...].reshape(count * cols, depth),
+            (((1,), (1,)), ((), ())),
+            preferred_element_type=jnp.float32,
+        )
+
+    mine, other = product(mine_ref), product(other_ref)
+    is_first = info_ref[0] % 2 == 0
+    pair = (jnp.where(is_first, mine, other), jnp.where(is_first, other, mine))
+    cols = mine_ref.shape[1]
+    mixed = jnp.concatenate(
+        [part[:, i * cols : (i + 1) * cols] for i in range(mine_ref.shape[0]) for part in pair], axis=1
     )
     out_ref[...] = (resid_ref[...].astype(jnp.float32) + mixed).astype(jnp.bfloat16)
 
 
-def feed_forward(attended, states, out_proj, norm_gain, up_proj, down_rows):
+def feed_forward(attended, states, out_proj, norm_gain, up_proj, down_mine):
     rows, width = states.shape
     units = up_proj.shape[1]
     step = math.gcd(units, 512)
     whole = lambda i: (0, 0)
+    seq_count = lax.axis_size("seq")
+    attended, down_mine = lax.optimization_barrier((attended, down_mine))
+    down_other = lax.ppermute(down_mine, "seq", [(i, i ^ 1) for i in range(seq_count)])
     resid, hidden = pl.pallas_call(
         lift_kernel,
         grid=(units // step,),
@@ -329,29 +344,38 @@
         ),
         name="project_and_lift",
     )(attended, states, out_proj, norm_gain.reshape(1, width), up_proj)
-    part = math.gcd(width, 256)
+    pairs = seq_count // 2
+    cols = width // seq_count
+    take = next(n for n in range(1, pairs + 1) if pairs % n == 0 and 2 * n * cols % 128 == 0)
+    weights = pl.BlockSpec((take, cols, units), lambda i: (i, 0, 0))
+    part = pl.BlockSpec((rows, 2 * take * cols), lambda i: (0, i))
     return pl.pallas_call(
         lower_kernel,
-        grid=(width // part,),
+        grid=(pairs // take,),
         out_shape=jax.ShapeDtypeStruct((rows, width), jnp.bfloat16),
         in_specs=[
+            pl.BlockSpec(memory_space=pltpu.SMEM),
             pl.BlockSpec((rows, units), whole),
-            pl.BlockSpec((part, units), lambda i: (i, 0)),
-            pl.BlockSpec((rows, part), lambda i: (0, i)),
+            weights,
+            weights,
+            part,
         ],
-        out_specs=pl.BlockSpec((rows, part), lambda i: (0, i)),
+        out_specs=part,
         compiler_params=pltpu.CompilerParams(vmem_limit_bytes=VMEM_BYTES),
         name="lower",
-    )(hidden, down_rows, resid)
+    )(lax.axis_index("seq").reshape(1).astype(jnp.int32), hidden, down_mine, down_other, resid)
 
 
 def per_device(states, query_rows, key_rows, value_rows, out_proj, norm_gain, up_proj, down_proj):
     model_width = states.shape[1]
     mp_pos = lax.axis_index("mp")
+    if lax.axis_size("mp") == 1:
+        same_core = [list(range(core, lax.axis_size("seq"), 2)) for core in range(2)]
+        down_mine = lax.all_gather(down_proj.T, "seq", axis=0, axis_index_groups=same_core)
+        attended = attention(query_rows, key_rows, value_rows)
+        return feed_forward(attended, states, out_proj, norm_gain, up_proj, down_mine)
     down_rows = lax.all_gather(down_proj.T, "seq", axis=0, tiled=True)
     attended = attention(query_rows, key_rows, value_rows)
-    if lax.axis_size("mp") == 1:
-        return feed_forward(attended, states, out_proj, norm_gain, up_proj, down_rows)
     projected = jnp.dot(attended, out_proj, preferred_element_type=jnp.float32)
     share = lax.psum_scatter(projected, "mp", scatter_dimension=1, tiled=True)
     half_width = share.shape[1]

time: 242 us -> 258 us (1.066)
  waiting for transfers between devices: 120 us -> 137 us
    all_gather x1, waiting for transfers between devices: 34.3 us -> 50.9 us  [per_device(): lax.all_gather(down_proj.T, 'seq', axis=0, axis_index_groups=same_core)]
    unnamed x17 -> x25, local copies, waits for them, and re-layouts: 9.44 us -> 10.4 us
  transfers between devices with their start and end apart: 7 -> 8, of which waited for: 5 -> 5; matrix products, arithmetic and copies ran while one was open for 5% -> 4% of each run, Pallas kernels for 22% -> 20%
where the time goes in v4:
time: 258 us; the launch traced here: 253 us
  waiting for transfers between devices  137 us (53%)
  Pallas kernels  65.9 us (26%)
  local copies, waits for them, and re-layouts  19.4 us (8%)
  starting transfers between devices  16.9 us (7%)
  between operations  13.7 us (5%)
    all_gather x1, waiting for transfers between devices, per_device(): lax.all_gather(down_proj.T, 'seq', axis=0, axis_index_groups=same_core)  50.9 us
    ppermute x3, waiting for transfers between devices, attention(): extras.append(lax.ppermute(flat[:, :stride // 2 ** tier], 'seq', pairs))  39.1 us
    all_to_all x1, waiting for transfers between devices, attention(): lax.all_to_all(packed.reshape(group, heads_dev, stride, per, SLAB), 'seq'...  32.5 us
    pallas_call x1, Pallas kernels, feed_forward(): pl.pallas_call(lift_kernel, grid=(units // step,), out_shape=(jax.ShapeDt...  17.4 us
    pallas_call x1, Pallas kernels, feed_forward(): pl.pallas_call(lower_kernel, grid=(pairs // take,), out_shape=jax.ShapeDt...  15.6 us
    pallas_call x1, Pallas kernels, attention(): pl.pallas_call(functools.partial(earlier_kernel, tiers, group), grid=(hea...  14.9 us
    pallas_call x1, Pallas kernels, attention(): pl.pallas_call(functools.partial(segment_kernel, tiers, heads_dev, group)...  14.9 us
    all_to_all x2, waiting for transfers between devices, send_home(): part = lax.all_to_all(part, 'seq', 0, 0, axis_index_groups=groups)  13.8 us
  transfers between devices with their start and end apart: 8, of which 5 were waited for; matrix products, arithmetic and copies ran while one was open for 4% of the time, Pallas kernels for 20%

profile of v4, /device:TPU:24, one launch (start us, length us, event | category | flops | bytes accessed | tf_op | source)
XLA Modules:
  0.0 253.3 jit_solution(132490359652835108)
XLA Ops:
  6.5 0.7 all-gather.3.cloned.1.call-update
  7.3 1.1 copy-done.4
  8.3 1.1 copy-done.5
  9.4 1.1 copy-done.6
  10.5 3.0 %pack_heads.1 = bf16[16,4,64,256]{3,2,1,0:T(8,128)(2,1)} custom-call(bf16[256,1280]{1,0:T(8,128)(2,1)S(1)} %copy-done.4, bf16[256,1280]{1,0:T(8,128)(2,1)S(1)} %copy-done.5, bf16[256,1280]{1,0:T(8,128)(2,1)S(1)} %copy-done.6), custom_call_target="tpu_custom_call" | custom-call | tf_op jit(solution)/shard_map/pack_heads/pallas_call | solution.py:186
  13.5 4.4 %all-to-all-start = ((bf16[8,2,4,64,256]{4,3,2,1,0:T(8,128)(2,1)}), bf16[8,2,4,64,256]{4,3,2,1,0:T(8,128)(2,1)}, u32[]{:S(2)}, u32[]{:S(2)}) async-start(bf16[8,2,4,64,256]{4,3,2,1,0:T(8,128)(2,1)} %bitcast.1), calls=%async_computation | async-start | bytes 4194304 | tf_op jit(solution)/shard_map/all_to_all | solution.py:196
  17.9 32.5 %all-to-all-done = bf16[8,2,4,64,256]{4,3,2,1,0:T(8,128)(2,1)} async-done(((bf16[8,2,4,64,256]{4,3,2,1,0:T(8,128)(2,1)}), bf16[8,2,4,64,256]{4,3,2,1,0:T(8,128)(2,1)}, u32[]{:S(2)}, u32[]{:S(2)}) %all-to-all-start) | async-done | bytes 2097184 | tf_op jit(solution)/shard_map/all_to_all | solution.py:196
  50.4 1.7 copy.37
  52.2 1.2 copy.42
  53.4 1.7 slice.274
  55.1 1.3 collective-permute-start.2
  56.4 1.3 collective-permute-start.1
  57.7 1.3 collective-permute-start
  59.0 14.9 %segment_attend.1 = (bf16[2,2,512,128]{3,2,1,0:T(8,128)(2,1)S(1)}, f32[2,2,512,256]{3,2,1,0:T(8,128)S(1)}, f32[2,2,512,128]{3,2,1,0:T(8,128)S(1)}) custom-call(s32[1]{0:T(128)} %bitcast.info_ref, bf16[2,4,512,256]{3,2,1,0:T(8,128)(2,1)S(1)} %bitcast.220), custom_call_target="tpu_custom_call" | custom-call | flops 8589934592 | bytes 6291456 | tf_op jit(solution)/shard_map/segment_attend/pallas_call | solution.py:223
  73.9 1.3 copy-done.1
  75.2 0.8 copy.45
  76.1 4.3 %all-to-all-start.2 = ((bf16[8,2,2,80,64]{3,4,2,1,0:T(8,128)(2,1)}), bf16[8,2,2,80,64]{3,4,2,1,0:T(8,128)(2,1)}, u32[]{:S(2)}, u32[]{:S(2)}) async-start(bf16[8,2,2,80,64]{3,4,2,1,0:T(8,128)(2,1)} %bitcast.226), calls=%async_computation.2 | async-start | bytes 1048576 | tf_op jit(solution)/shard_map/all_to_all | solution.py:247
  80.4 32.8 %collective-permute-done.1.rest_1_ = bf16[2,1,160,512]{3,2,1,0:T(8,128)(2,1)} collective-permute-done((bf16[2,1,160,512]{3,2,1,0:T(8,128)(2,1)}, bf16[2,1,160,512]{3,2,1,0:T(8,128)(2,1)}, u32[]{:S(2)}, u32[]{:S(2)}) %collective-permute-start.1) | collective-permute-done | bytes 327712 | tf_op jit(solution)/shard_map/ppermute | solution.py:212
  113.2 6.3 %collective-permute-done.rest_0_ = bf16[2,2,160,512]{3,2,1,0:T(8,128)(2,1)} collective-permute-done((bf16[2,2,160,512]{3,2,1,0:T(8,128)(2,1)}, bf16[2,2,160,512]{3,2,1,0:T(8,128)(2,1)}, u32[]{:S(2)}, u32[]{:S(2)}) %collective-permute-start) | collective-permute-done | bytes 655392 | tf_op jit(solution)/shard_map/ppermute | solution.py:212
  119.5 1.6 copy-done.2
  121.1 14.9 %earlier_segments.1 = bf16[2,2,512,128]{3,2,1,0:T(8,128)(2,1)S(1)} custom-call(s32[1]{0:T(128)} %bitcast.info_ref, bf16[2,4,512,256]{3,2,1,0:T(8,128)(2,1)S(1)} %bitcast.221, f32[2,2,512,256]{3,2,1,0:T(8,128)S(1)} %copy-done.2, f32[2,2,512,128]{3,2,1,0:T(8,128)S(1)} %get-tuple-element.13.peak_in, bf16[2,2,160,512]{3,2,1,0:T(8,128)(2,1)} %collective-permute-done.rest_0_, ...), custom_call_target="tpu_custom_call" | custom-call | tf_op jit(solution)/shard_map/earlier_segments/pallas_call | solution.py:251
  136.0 0.8 copy.46
  136.9 4.3 %all-to-all-start.1 = ((bf16[8,2,2,80,64]{3,4,2,1,0:T(8,128)(2,1)}), bf16[8,2,2,80,64]{3,4,2,1,0:T(8,128)(2,1)S(1)}, u32[]{:S(2)}, u32[]{:S(2)}) async-start(bf16[8,2,2,80,64]{3,4,2,1,0:T(8,128)(2,1)} %bitcast.212), calls=%async_computation.1 | async-start | bytes 1048576 | tf_op jit(solution)/shard_map/all_to_all | solution.py:247
  141.2 0.9 slice_bitcast_fusion.38
  142.1 0.9 slice_bitcast_fusion.3
  143.0 13.8 %all-to-all-done.1 = bf16[8,2,2,80,64]{3,4,2,1,0:T(8,128)(2,1)S(1)} async-done(((bf16[8,2,2,80,64]{3,4,2,1,0:T(8,128)(2,1)}), bf16[8,2,2,80,64]{3,4,2,1,0:T(8,128)(2,1)S(1)}, u32[]{:S(2)}, u32[]{:S(2)}) %all-to-all-start.1) | async-done | bytes 327712 | tf_op jit(solution)/shard_map/all_to_all | solution.py:247
  157.4 0.7 copy.41
  158.1 1.2 reshape.35.att_ref
  159.3 50.9 %all-gather.3.cloned.1.call-done = bf16[1280,5120]{1,0:T(8,128)(2,1)} async-done(((bf16[80,5120]{1,0:T(8,128)(2,1)}), bf16[1280,5120]{1,0:T(8,128)(2,1)}) %all-gather.3.cloned.1.call-update) | async-done | bytes 13107216 | tf_op jit(solution)/shard_map/all_gather | solution.py:374
  210.3 3.0 %copy-done = bf16[1280,2560]{1,0:T(8,128)(2,1)S(1)} copy-done((bf16[1280,2560]{1,0:T(8,128)(2,1)S(1)}, bf16[1280,2560]{1,0:T(8,128)(2,1)}, u32[]{:S(2)}) %copy-start) | copy-done | bytes 6553624
  213.3 17.4 %project_and_lift.1 = (bf16[256,2560]{1,0:T(8,128)(2,1)S(1)}, bf16[256,5120]{1,0:T(8,128)(2,1)S(1)}) custom-call(bf16[256,1280]{1,0:T(8,128)(2,1)S(1)} %reshape.35.att_ref, bf16[256,2560]{1,0:T(8,128)(2,1)S(1)} %copy-done.3, bf16[1280,2560]{1,0:T(8,128)(2,1)S(1)} %copy-done, f32[1,2560]{1,0:T(1,128)S(1)} %reshape.36.gain_ref, bf16[2560,5120]{1,0:T(8,128)(2,1)} %up_ref.1), custom_call_target="tpu_custom_call" | custom-call | flops 8388608000 | bytes 32768000 | tf_op jit(solution)/shard_map/project_and_lift/pallas_call | solution.py:320
  230.8 15.6 %lower.1 = bf16[256,2560]{1,0:T(8,128)(2,1)} custom-call(s32[1]{0:T(128)} %bitcast.info_ref, bf16[256,5120]{1,0:T(8,128)(2,1)S(1)} %get-tuple-element.16.hidden_ref, bf16[16,80,5120]{2,1,0:T(8,128)(2,1)S(1)} %bitcast.218, bf16[16,80,5120]{2,1,0:T(8,128)(2,1)} %collective-permute-done.3.other_ref, bf16[256,2560]{1,0:T(8,128)(2,1)S(1)} %get-tuple-element.18.resid_ref), custom_call_target="tpu_custom_call" | custom-call | tf_op jit(solution)/shard_map/lower/pallas_call | solution.py:352
  (44 shorter events, 0.7 us)
Async XLA Ops:
  6.5 203.6 %all-gather.3.cloned.1.call-start = ((), (), s32[]{:S(2)}) async-start(), calls=%async_computation.3 | async-start | bytes 13926400 | tf_op jit(solution)/shard_map/all_gather | solution.py:374
  7.3 1.1 copy-start.4
  8.3 1.1 copy-start.5
  9.4 1.1 copy-start.6
  13.5 36.8 %all-to-all-start = ((bf16[8,2,4,64,256]{4,3,2,1,0:T(8,128)(2,1)}), bf16[8,2,4,64,256]{4,3,2,1,0:T(8,128)(2,1)}, u32[]{:S(2)}, u32[]{:S(2)}) async-start(bf16[8,2,4,64,256]{4,3,2,1,0:T(8,128)(2,1)} %bitcast.1), calls=%async_computation | async-start | bytes 4194304 | tf_op jit(solution)/shard_map/all_to_all | solution.py:196
  55.1 25.3 %collective-permute-start.2 = (bf16[2,1,160,512]{3,2,1,0:T(8,128)(2,1)}, bf16[2,1,160,512]{3,2,1,0:T(8,128)(2,1)S(1)}, u32[]{:S(2)}, u32[]{:S(2)}) collective-permute-start(bf16[2,1,160,512]{3,2,1,0:T(8,128)(2,1)} %slice.274), channel_id=1, source_target_pairs={{0,24},{1,25},{2,26},{3,27},{4,28},{5,29},{6,30},{7,31},{8,16},{9,... | collective-permute-start | bytes 983048 | tf_op jit(solution)/shard_map/ppermute | solution.py:212
  56.4 56.8 %collective-permute-start.1 = (bf16[2,1,160,512]{3,2,1,0:T(8,128)(2,1)}, bf16[2,1,160,512]{3,2,1,0:T(8,128)(2,1)}, u32[]{:S(2)}, u32[]{:S(2)}) collective-permute-start(bf16[2,1,160,512]{3,2,1,0:T(8,128)(2,1)} %slice.274), channel_id=1, source_target_pairs={{0,16},{1,17},{2,18},{3,19},{4,20},{5,21},{6,22},{7,23},{8,24},{9,... | collective-permute-start | bytes 983048 | tf_op jit(solution)/shard_map/ppermute | solution.py:212
  57.7 61.8 %collective-permute-start = (bf16[2,2,160,512]{3,2,1,0:T(8,128)(2,1)}, bf16[2,2,160,512]{3,2,1,0:T(8,128)(2,1)}, u32[]{:S(2)}, u32[]{:S(2)}) collective-permute-start(bf16[2,2,160,512]{3,2,1,0:T(8,128)(2,1)} %bitcast.228), channel_id=1, source_target_pairs={{0,8},{1,9},{2,10},{3,11},{4,12},{5,13},{6,14},{7,15},{16,24},{17,... | collective-permute-start | bytes 1966088 | tf_op jit(solution)/shard_map/ppermute | solution.py:212
  73.9 1.3 copy-start.1
  76.1 60.8 %all-to-all-start.2 = ((bf16[8,2,2,80,64]{3,4,2,1,0:T(8,128)(2,1)}), bf16[8,2,2,80,64]{3,4,2,1,0:T(8,128)(2,1)}, u32[]{:S(2)}, u32[]{:S(2)}) async-start(bf16[8,2,2,80,64]{3,4,2,1,0:T(8,128)(2,1)} %bitcast.226), calls=%async_computation.2 | async-start | bytes 1048576 | tf_op jit(solution)/shard_map/all_to_all | solution.py:247
  119.5 1.6 copy-start.2
  136.9 20.0 %all-to-all-start.1 = ((bf16[8,2,2,80,64]{3,4,2,1,0:T(8,128)(2,1)}), bf16[8,2,2,80,64]{3,4,2,1,0:T(8,128)(2,1)S(1)}, u32[]{:S(2)}, u32[]{:S(2)}) async-start(bf16[8,2,2,80,64]{3,4,2,1,0:T(8,128)(2,1)} %bitcast.212), calls=%async_computation.1 | async-start | bytes 1048576 | tf_op jit(solution)/shard_map/all_to_all | solution.py:247
  157.3 52.9 %copy-start.7 = (f32[2560]{0:T(1024)S(1)}, f32[2560]{0:T(1024)}, u32[]{:S(2)}) copy-start(f32[2560]{0:T(1024)} %param.13) | copy-start | bytes 30724
  157.3 52.9 %copy-start.3 = (bf16[256,2560]{1,0:T(8,128)(2,1)S(1)}, bf16[256,2560]{1,0:T(8,128)(2,1)}, u32[]{:S(2)}) copy-start(bf16[256,2560]{1,0:T(8,128)(2,1)} %states_ref.1) | copy-start | bytes 3932164
  210.2 20.5 %collective-permute-start.3 = (bf16[16,80,5120]{2,1,0:T(8,128)(2,1)}, bf16[16,80,5120]{2,1,0:T(8,128)(2,1)}, u32[]{:S(2)}, u32[]{:S(2)}) collective-permute-start(bf16[16,80,5120]{2,1,0:T(8,128)(2,1)} %bitcast.215), channel_id=1, source_target_pairs={{0,1},{1,0},{2,3},{3,2},{4,5},{5,4},{6,7},{7,6},{8,9},{9,8},{10,11... | collective-permute-start | bytes 39321608 | tf_op jit(solution)/shard_map/ppermute | solution.py:319
  210.2 20.5 %slice-start = ((s8[13107200]{0:T(1024)(128)(4,1)}), s8[4194304]{0:T(1024)(128)(4,1)S(1)}, s32[]{:S(2)}) async-start(s8[13107200]{0:T(1024)(128)(4,1)} %bitcast.216), calls=%async_computation.4 | async-start | bytes 8388608
  210.3 3.0 %copy-start = (bf16[1280,2560]{1,0:T(8,128)(2,1)S(1)}, bf16[1280,2560]{1,0:T(8,128)(2,1)}, u32[]{:S(2)}) copy-start(bf16[1280,2560]{1,0:T(8,128)(2,1)} %proj_ref.1) | copy-start | bytes 19660804
  213.3 17.5 %slice-start.1 = ((s8[13107200]{0:T(1024)(128)(4,1)}), s8[4194304]{0:T(1024)(128)(4,1)S(1)}, s32[]{:S(2)}) async-start(s8[13107200]{0:T(1024)(128)(4,1)} %bitcast.216), calls=%async_computation.5 | async-start | bytes 8388608
  213.3 17.5 %slice-start.2 = ((s8[13107200]{0:T(1024)(128)(4,1)}), s8[4194304]{0:T(1024)(128)(4,1)S(1)}, s32[]{:S(2)}) async-start(s8[13107200]{0:T(1024)(128)(4,1)} %bitcast.216), calls=%async_computation.6 | async-start | bytes 8388608
  213.3 17.5 %slice-start.3 = ((s8[13107200]{0:T(1024)(128)(4,1)}), s8[524288]{0:T(1024)(128)(4,1)S(1)}, s32[]{:S(2)}) async-start(s8[13107200]{0:T(1024)(128)(4,1)} %bitcast.216), calls=%async_computation.7 | async-start | bytes 1048576
Sparse Core Ops, SparseCore 0:
  10.1 200.0 all-gather.2

commit v5 on v3

--- a/solution.py
+++ b/solution.py
@@ -14,7 +14,8 @@
 ONES_AT = 3 * HEAD_DIM
 CHUNK = 128
 MASKED = -1e30
-VMEM_BYTES = 48 * 1024 * 1024
+VMEM_BYTES = 30 * 1024 * 1024
+PARTS = 2
 
 
 def reversed_bits(value, bits):
@@ -287,17 +288,17 @@
     hidden_ref[...] = (0.5 * raw * (1.0 + lax.erf(raw * math.sqrt(0.5)))).astype(jnp.bfloat16)
 
 
-def lower_kernel(hidden_ref, down_ref, resid_ref, out_ref):
+def lower_kernel(hidden_ref, down_ref, before_ref, out_ref):
     mixed = lax.dot_general(
         hidden_ref[...],
         down_ref[...],
         (((1,), (1,)), ((), ())),
         preferred_element_type=jnp.float32,
     )
-    out_ref[...] = (resid_ref[...].astype(jnp.float32) + mixed).astype(jnp.bfloat16)
-
-
-def feed_forward(attended, states, out_proj, norm_gain, up_proj, down_rows):
+    out_ref[...] = (before_ref[...].astype(jnp.float32) + mixed).astype(out_ref.dtype)
+
+
+def feed_forward(attended, states, out_proj, norm_gain, up_proj, down_parts):
     rows, width = states.shape
     units = up_proj.shape[1]
     step = math.gcd(units, 512)
@@ -330,28 +331,45 @@
         name="project_and_lift",
     )(attended, states, out_proj, norm_gain.reshape(1, width), up_proj)
     part = math.gcd(width, 256)
-    return pl.pallas_call(
-        lower_kernel,
-        grid=(width // part,),
-        out_shape=jax.ShapeDtypeStruct((rows, width), jnp.bfloat16),
-        in_specs=[
-            pl.BlockSpec((rows, units), whole),
-            pl.BlockSpec((part, units), lambda i: (i, 0)),
-            pl.BlockSpec((rows, part), lambda i: (0, i)),
-        ],
-        out_specs=pl.BlockSpec((rows, part), lambda i: (0, i)),
-        compiler_params=pltpu.CompilerParams(vmem_limit_bytes=VMEM_BYTES),
-        name="lower",
-    )(hidden, down_rows, resid)
+    total, start = resid, 0
+    for down_part in down_parts:
+        depth = down_part.shape[1]
+        last = start + depth == units
+        block, kept = start // depth, jnp.bfloat16 if last else jnp.float32
+        total = pl.pallas_call(
+            lower_kernel,
+            grid=(width // part,),
+            out_shape=jax.ShapeDtypeStruct((rows, width), kept),
+            in_specs=[
+                pl.BlockSpec((rows, depth), lambda i, block=block: (0, block)),
+                pl.BlockSpec((part, depth), lambda i: (i, 0)),
+                pl.BlockSpec((rows, part), lambda i: (0, i)),
+            ],
+            out_specs=pl.BlockSpec((rows, part), lambda i: (0, i)),
+            compiler_params=pltpu.CompilerParams(vmem_limit_bytes=VMEM_BYTES),
+            cost_estimate=pl.CostEstimate(
+                flops=2 * rows * width * depth, bytes_accessed=2 * width * depth, transcendentals=0
+            ),
+            name="lower",
+        )(hidden, down_part, total)
+        start += depth
+    return total
 
 
 def per_device(states, query_rows, key_rows, value_rows, out_proj, norm_gain, up_proj, down_proj):
     model_width = states.shape[1]
     mp_pos = lax.axis_index("mp")
+    if lax.axis_size("mp") == 1:
+        depth = down_proj.shape[0]
+        parts = PARTS if depth % (PARTS * 128) == 0 else 1
+        down_parts = [
+            lax.all_gather(rows, "seq", axis=0, tiled=True)
+            for rows in jnp.split(down_proj.T, parts, axis=1)
+        ]
+        attended = attention(query_rows, key_rows, value_rows)
+        return feed_forward(attended, states, out_proj, norm_gain, up_proj, down_parts)
     down_rows = lax.all_gather(down_proj.T, "seq", axis=0, tiled=True)
     attended = attention(query_rows, key_rows, value_rows)
-    if lax.axis_size("mp") == 1:
-        return feed_forward(attended, states, out_proj, norm_gain, up_proj, down_rows)
     projected = jnp.dot(attended, out_proj, preferred_element_type=jnp.float32)
     share = lax.psum_scatter(projected, "mp", scatter_dimension=1, tiled=True)
     half_width = share.shape[1]

time: 242 us -> 259 us (1.070)
  local copies, waits for them, and re-layouts: 18.6 us -> 34.6 us
  waiting for transfers between devices: 120 us -> 127 us
  Pallas kernels: 68.3 us -> 63.1 us
    all_gather x1 -> x2, waiting for transfers between devices: 34.3 us -> 65 us  [per_device(): lax.all_gather(rows, 'seq', axis=0, tiled=True)]
    ppermute x3, waiting for transfers between devices: 38.9 us -> 23.9 us  [attention(): extras.append(lax.ppermute(flat[:, :stride // 2 ** tier], 'seq', pairs))]
    unnamed x17 -> x29, local copies, waits for them, and re-layouts: 9.44 us -> 23.4 us
    all_to_all x2, waiting for transfers between devices: 13.8 us -> 7.83 us  [send_home(): part = lax.all_to_all(part, 'seq', 0, 0, axis_index_groups=groups)]
    pallas_call x1 -> x2, Pallas kernels: 15.5 us -> 12.6 us  [feed_forward(): pl.pallas_call(lower_kernel, grid=(width // part,), out_shape=jax.ShapeDt...]
    all_to_all x1, waiting for transfers between devices: 32.5 us -> 29.6 us  [attention(): lax.all_to_all(packed.reshape(group, heads_dev, stride, per, SLAB), 'seq'...]
  transfers between devices with their start and end apart: 7 -> 8, of which waited for: 5 -> 5; matrix products, arithmetic and copies ran while one was open for 5% -> 4% of each run, Pallas kernels for 22% -> 22%
where the time goes in v5:
time: 259 us; the launch traced here: 255 us
  waiting for transfers between devices  127 us (49%)
  Pallas kernels  63.1 us (24%)
  local copies, waits for them, and re-layouts  34.6 us (13%)
  starting transfers between devices  16.1 us (6%)
  between operations  13.7 us (5%)
    all_gather x2, waiting for transfers between devices, per_device(): lax.all_gather(rows, 'seq', axis=0, tiled=True)  65 us
    all_to_all x1, waiting for transfers between devices, attention(): lax.all_to_all(packed.reshape(group, heads_dev, stride, per, SLAB), 'seq'...  29.6 us
    ppermute x3, waiting for transfers between devices, attention(): extras.append(lax.ppermute(flat[:, :stride // 2 ** tier], 'seq', pairs))  23.9 us
    unnamed x29, local copies, waits for them, and re-layouts  23.4 us
    pallas_call x1, Pallas kernels, feed_forward(): pl.pallas_call(lift_kernel, grid=(units // step,), out_shape=(jax.ShapeDt...  17.4 us
    pallas_call x1, Pallas kernels, attention(): pl.pallas_call(functools.partial(segment_kernel, tiers, heads_dev, group)...  15.1 us
    pallas_call x1, Pallas kernels, attention(): pl.pallas_call(functools.partial(earlier_kernel, tiers, group), grid=(hea...  14.9 us
    pallas_call x2, Pallas kernels, feed_forward(): pl.pallas_call(lower_kernel, grid=(width // part,), out_shape=jax.ShapeDt...  12.6 us
  transfers between devices with their start and end apart: 8, of which 5 were waited for; matrix products, arithmetic and copies ran while one was open for 4% of the time, Pallas kernels for 22%

profile of v5, /device:TPU:24, one launch (start us, length us, event | category | flops | bytes accessed | tf_op | source)
XLA Modules:
  0.0 254.8 jit_solution(4362519981967910846)
XLA Ops:
  6.5 2.2 fusion.16
  9.6 3.1 %pack_heads.1 = bf16[16,4,64,256]{3,2,1,0:T(8,128)(2,1)} custom-call(bf16[256,1280]{1,0:T(8,128)(2,1)S(1)} %copy-done.10, bf16[256,1280]{1,0:T(8,128)(2,1)S(1)} %copy-done.11, bf16[256,1280]{1,0:T(8,128)(2,1)S(1)} %copy-done.12), custom_call_target="tpu_custom_call" | custom-call | tf_op jit(solution)/shard_map/pack_heads/pallas_call | solution.py:187
  12.6 4.4 %all-to-all-start = ((bf16[8,2,4,64,256]{4,3,2,1,0:T(8,128)(2,1)}), bf16[8,2,4,64,256]{4,3,2,1,0:T(8,128)(2,1)}, u32[]{:S(2)}, u32[]{:S(2)}) async-start(bf16[8,2,4,64,256]{4,3,2,1,0:T(8,128)(2,1)} %bitcast.1), calls=%async_computation | async-start | bytes 4194304 | tf_op jit(solution)/shard_map/all_to_all | solution.py:197
  17.0 29.6 %all-to-all-done = bf16[8,2,4,64,256]{4,3,2,1,0:T(8,128)(2,1)} async-done(((bf16[8,2,4,64,256]{4,3,2,1,0:T(8,128)(2,1)}), bf16[8,2,4,64,256]{4,3,2,1,0:T(8,128)(2,1)}, u32[]{:S(2)}, u32[]{:S(2)}) %all-to-all-start) | async-done | bytes 2097184 | tf_op jit(solution)/shard_map/all_to_all | solution.py:197
  46.6 1.7 copy.37
  48.4 1.2 copy.42
  49.6 1.7 slice.274
  51.3 1.3 collective-permute-start.1
  52.6 1.3 collective-permute-start.2
  53.9 1.3 collective-permute-start
  55.2 15.1 %segment_attend.1 = (bf16[2,2,512,128]{3,2,1,0:T(8,128)(2,1)S(1)}, f32[2,2,512,256]{3,2,1,0:T(8,128)S(1)}, f32[2,2,512,128]{3,2,1,0:T(8,128)S(1)}) custom-call(s32[1]{0:T(128)} %bitcast.info_ref, bf16[2,4,512,256]{3,2,1,0:T(8,128)(2,1)S(1)} %bitcast.215), custom_call_target="tpu_custom_call" | custom-call | flops 8589934592 | bytes 6291456 | tf_op jit(solution)/shard_map/segment_attend/pallas_call | solution.py:224
  70.3 1.3 copy-done.5
  72.5 4.3 %all-to-all-start.2 = ((bf16[8,2,2,80,64]{3,4,2,1,0:T(8,128)(2,1)}), bf16[8,2,2,80,64]{3,4,2,1,0:T(8,128)(2,1)}, u32[]{:S(2)}, u32[]{:S(2)}) async-start(bf16[8,2,2,80,64]{3,4,2,1,0:T(8,128)(2,1)} %bitcast.221), calls=%async_computation.2 | async-start | bytes 1048576 | tf_op jit(solution)/shard_map/all_to_all | solution.py:248
  76.8 7.6 %collective-permute-done.1.rest_1_ = bf16[2,1,160,512]{3,2,1,0:T(8,128)(2,1)S(1)} collective-permute-done((bf16[2,1,160,512]{3,2,1,0:T(8,128)(2,1)}, bf16[2,1,160,512]{3,2,1,0:T(8,128)(2,1)S(1)}, u32[]{:S(2)}, u32[]{:S(2)}) %collective-permute-start.1) | collective-permute-done | bytes 327712 | tf_op jit(solution)/shard_map/ppermute | solution.py:213
  84.5 16.3 %collective-permute-done.rest_0_ = bf16[2,2,160,512]{3,2,1,0:T(8,128)(2,1)} collective-permute-done((bf16[2,2,160,512]{3,2,1,0:T(8,128)(2,1)}, bf16[2,2,160,512]{3,2,1,0:T(8,128)(2,1)}, u32[]{:S(2)}, u32[]{:S(2)}) %collective-permute-start) | collective-permute-done | bytes 655392 | tf_op jit(solution)/shard_map/ppermute | solution.py:213
  100.7 1.6 copy-done.6
  102.3 14.9 %earlier_segments.1 = bf16[2,2,512,128]{3,2,1,0:T(8,128)(2,1)S(1)} custom-call(s32[1]{0:T(128)} %bitcast.info_ref, bf16[2,4,512,256]{3,2,1,0:T(8,128)(2,1)S(1)} %bitcast.216, f32[2,2,512,256]{3,2,1,0:T(8,128)S(1)} %copy-done.6, f32[2,2,512,128]{3,2,1,0:T(8,128)S(1)} %get-tuple-element.11.peak_in, bf16[2,2,160,512]{3,2,1,0:T(8,128)(2,1)} %collective-permute-done.rest_0_, ...), custom_call_target="tpu_custom_call" | custom-call | tf_op jit(solution)/shard_map/earlier_segments/pallas_call | solution.py:252
  118.1 3.5 %all-to-all-start.1 = ((bf16[8,2,2,80,64]{3,4,2,1,0:T(8,128)(2,1)}), bf16[8,2,2,80,64]{3,4,2,1,0:T(8,128)(2,1)S(1)}, u32[]{:S(2)}, u32[]{:S(2)}) async-start(bf16[8,2,2,80,64]{3,4,2,1,0:T(8,128)(2,1)} %bitcast.211), calls=%async_computation.1 | async-start | bytes 1048576 | tf_op jit(solution)/shard_map/all_to_all | solution.py:248
  123.4 7.8 %all-to-all-done.1 = bf16[8,2,2,80,64]{3,4,2,1,0:T(8,128)(2,1)S(1)} async-done(((bf16[8,2,2,80,64]{3,4,2,1,0:T(8,128)(2,1)}), bf16[8,2,2,80,64]{3,4,2,1,0:T(8,128)(2,1)S(1)}, u32[]{:S(2)}, u32[]{:S(2)}) %all-to-all-start.1) | async-done | bytes 327712 | tf_op jit(solution)/shard_map/all_to_all | solution.py:248
  132.5 1.2 reshape.34.att_ref
  133.7 2.9 %copy-done.4 = bf16[1280,2560]{1,0:T(8,128)(2,1)S(1)} copy-done((bf16[1280,2560]{1,0:T(8,128)(2,1)S(1)}, bf16[1280,2560]{1,0:T(8,128)(2,1)}, u32[]{:S(2)}) %copy-start.4) | copy-done | bytes 6553624
  136.6 1.3 copy-done.7
  137.9 17.4 %project_and_lift.1 = (bf16[256,2560]{1,0:T(8,128)(2,1)S(1)}, bf16[256,5120]{1,0:T(8,128)(2,1)S(1)}) custom-call(bf16[256,1280]{1,0:T(8,128)(2,1)S(1)} %reshape.34.att_ref, bf16[256,2560]{1,0:T(8,128)(2,1)S(1)} %copy-done.7, bf16[1280,2560]{1,0:T(8,128)(2,1)S(1)} %copy-done.4, f32[1,2560]{1,0:T(1,128)S(1)} %reshape.35.gain_ref, bf16[2560,5120]{1,0:T(8,128)(2,1)} %up_ref.1), custom_call_target="tpu_custom_call" | custom-call | flops 8388608000 | bytes 32768000 | tf_op jit(solution)/shard_map/project_and_lift/pallas_call | solution.py:306
  155.3 1.0 copy-done.8
  156.4 4.7 %copy-done = bf16[2560,2560]{1,0:T(8,128)(2,1)S(1)} copy-done((bf16[2560,2560]{1,0:T(8,128)(2,1)S(1)}, bf16[2560,2560]{1,0:T(8,128)(2,1)}, u32[]{:S(2)}) %copy-start) | copy-done | bytes 13107224
  161.1 1.3 copy-done.9
  162.5 5.8 %lower.2.before_ref = f32[256,2560]{1,0:T(8,128)S(1)} custom-call(bf16[256,5120]{1,0:T(8,128)(2,1)S(1)} %get-tuple-element.13.hidden_ref, bf16[2560,2560]{1,0:T(8,128)(2,1)S(1)} %copy-done, bf16[256,2560]{1,0:T(8,128)(2,1)S(1)} %copy-done.9), custom_call_target="tpu_custom_call" | custom-call | flops 3355443200 | bytes 13107200 | tf_op jit(solution)/shard_map/lower/pallas_call | solution.py:339
  168.3 1.5 copy-done.2
  169.8 65.0 %all-gather.3.cloned.1.call-done.down_ref = bf16[2560,2560]{1,0:T(8,128)(2,1)} async-done(((bf16[80,2560]{1,0:T(8,128)(2,1)}), bf16[2560,2560]{1,0:T(8,128)(2,1)}) %all-gather.3.cloned.1.call-update) | async-done | bytes 13107216 | tf_op jit(solution)/shard_map/all_gather | solution.py:366
  234.8 4.7 %copy-done.1 = bf16[2560,2560]{1,0:T(8,128)(2,1)S(1)} copy-done((bf16[2560,2560]{1,0:T(8,128)(2,1)S(1)}, bf16[2560,2560]{1,0:T(8,128)(2,1)}, u32[]{:S(2)}) %copy-start.1) | copy-done | bytes 13107224
  239.5 1.7 copy-done.3
  241.2 6.7 %lower.3 = bf16[256,2560]{1,0:T(8,128)(2,1)} custom-call(bf16[256,5120]{1,0:T(8,128)(2,1)S(1)} %get-tuple-element.13.hidden_ref, bf16[2560,2560]{1,0:T(8,128)(2,1)S(1)} %copy-done.1, f32[256,2560]{1,0:T(8,128)S(1)} %copy-done.3), custom_call_target="tpu_custom_call" | custom-call | flops 3355443200 | bytes 13107200 | tf_op jit(solution)/shard_map/lower/pallas_call | solution.py:339
  (50 shorter events, 5.6 us)
Async XLA Ops:
  6.5 3.0 %copy-start.11 = (bf16[256,1280]{1,0:T(8,128)(2,1)S(1)}, bf16[256,1280]{1,0:T(8,128)(2,1)}, u32[]{:S(2)}) copy-start(bf16[256,1280]{1,0:T(8,128)(2,1)} %k_ref.1) | copy-start | bytes 1966084
  6.5 3.0 %copy-start.12 = (bf16[256,1280]{1,0:T(8,128)(2,1)S(1)}, bf16[256,1280]{1,0:T(8,128)(2,1)}, u32[]{:S(2)}) copy-start(bf16[256,1280]{1,0:T(8,128)(2,1)} %v_ref.1) | copy-start | bytes 1966084
  6.5 3.0 %copy-start.10 = (bf16[256,1280]{1,0:T(8,128)(2,1)S(1)}, bf16[256,1280]{1,0:T(8,128)(2,1)}, u32[]{:S(2)}) copy-start(bf16[256,1280]{1,0:T(8,128)(2,1)} %q_ref.1) | copy-start | bytes 1966084
  6.5 149.8 %all-gather.5.cloned.1.call-start = ((), (), s32[]{:S(2)}) async-start(), calls=%async_computation.4 | async-start | bytes 13516800 | tf_op jit(solution)/shard_map/all_gather | solution.py:366
  8.8 226.0 %all-gather.3.cloned.1.call-start = ((), (), s32[]{:S(2)}) async-start(), calls=%async_computation.3 | async-start | bytes 13516800 | tf_op jit(solution)/shard_map/all_gather | solution.py:366
  12.6 34.0 %all-to-all-start = ((bf16[8,2,4,64,256]{4,3,2,1,0:T(8,128)(2,1)}), bf16[8,2,4,64,256]{4,3,2,1,0:T(8,128)(2,1)}, u32[]{:S(2)}, u32[]{:S(2)}) async-start(bf16[8,2,4,64,256]{4,3,2,1,0:T(8,128)(2,1)} %bitcast.1), calls=%async_computation | async-start | bytes 4194304 | tf_op jit(solution)/shard_map/all_to_all | solution.py:197
  51.3 33.1 %collective-permute-start.1 = (bf16[2,1,160,512]{3,2,1,0:T(8,128)(2,1)}, bf16[2,1,160,512]{3,2,1,0:T(8,128)(2,1)S(1)}, u32[]{:S(2)}, u32[]{:S(2)}) collective-permute-start(bf16[2,1,160,512]{3,2,1,0:T(8,128)(2,1)} %slice.274), channel_id=1, source_target_pairs={{0,16},{1,17},{2,18},{3,19},{4,20},{5,21},{6,22},{7,23},{8,24},{9,... | collective-permute-start | bytes 983048 | tf_op jit(solution)/shard_map/ppermute | solution.py:213
  52.6 31.8 %collective-permute-start.2 = (bf16[2,1,160,512]{3,2,1,0:T(8,128)(2,1)}, bf16[2,1,160,512]{3,2,1,0:T(8,128)(2,1)}, u32[]{:S(2)}, u32[]{:S(2)}) collective-permute-start(bf16[2,1,160,512]{3,2,1,0:T(8,128)(2,1)} %slice.274), channel_id=1, source_target_pairs={{0,24},{1,25},{2,26},{3,27},{4,28},{5,29},{6,30},{7,31},{8,16},{9,... | collective-permute-start | bytes 983048 | tf_op jit(solution)/shard_map/ppermute | solution.py:213
  53.9 46.8 %collective-permute-start = (bf16[2,2,160,512]{3,2,1,0:T(8,128)(2,1)}, bf16[2,2,160,512]{3,2,1,0:T(8,128)(2,1)}, u32[]{:S(2)}, u32[]{:S(2)}) collective-permute-start(bf16[2,2,160,512]{3,2,1,0:T(8,128)(2,1)} %bitcast.223), channel_id=1, source_target_pairs={{0,8},{1,9},{2,10},{3,11},{4,12},{5,13},{6,14},{7,15},{16,24},{17,... | collective-permute-start | bytes 1966088 | tf_op jit(solution)/shard_map/ppermute | solution.py:213
  70.3 1.3 copy-start.5
  71.6 5.2 %copy-start.13 = (f32[2560]{0:T(1024)S(1)}, f32[2560]{0:T(1024)}, u32[]{:S(2)}) copy-start(f32[2560]{0:T(1024)} %param.13) | copy-start | bytes 30724
  72.5 45.6 %all-to-all-start.2 = ((bf16[8,2,2,80,64]{3,4,2,1,0:T(8,128)(2,1)}), bf16[8,2,2,80,64]{3,4,2,1,0:T(8,128)(2,1)}, u32[]{:S(2)}, u32[]{:S(2)}) async-start(bf16[8,2,2,80,64]{3,4,2,1,0:T(8,128)(2,1)} %bitcast.221), calls=%async_computation.2 | async-start | bytes 1048576 | tf_op jit(solution)/shard_map/all_to_all | solution.py:248
  100.7 1.6 copy-start.6
  118.1 13.2 %all-to-all-start.1 = ((bf16[8,2,2,80,64]{3,4,2,1,0:T(8,128)(2,1)}), bf16[8,2,2,80,64]{3,4,2,1,0:T(8,128)(2,1)S(1)}, u32[]{:S(2)}, u32[]{:S(2)}) async-start(bf16[8,2,2,80,64]{3,4,2,1,0:T(8,128)(2,1)} %bitcast.211), calls=%async_computation.1 | async-start | bytes 1048576 | tf_op jit(solution)/shard_map/all_to_all | solution.py:248
  133.7 2.9 %copy-start.4 = (bf16[1280,2560]{1,0:T(8,128)(2,1)S(1)}, bf16[1280,2560]{1,0:T(8,128)(2,1)}, u32[]{:S(2)}) copy-start(bf16[1280,2560]{1,0:T(8,128)(2,1)} %proj_ref.1) | copy-start | bytes 19660804
  136.6 1.3 copy-start.7
  155.3 1.1 copy-start.8
  156.4 4.7 %copy-start = (bf16[2560,2560]{1,0:T(8,128)(2,1)S(1)}, bf16[2560,2560]{1,0:T(8,128)(2,1)}, u32[]{:S(2)}) copy-start(bf16[2560,2560]{1,0:T(8,128)(2,1)} %all-gather.5.cloned.1.call-done.down_ref) | copy-start | bytes 39321604
  161.1 1.3 copy-start.9
  168.3 1.5 copy-start.2
  234.8 4.7 %copy-start.1 = (bf16[2560,2560]{1,0:T(8,128)(2,1)S(1)}, bf16[2560,2560]{1,0:T(8,128)(2,1)}, u32[]{:S(2)}) copy-start(bf16[2560,2560]{1,0:T(8,128)(2,1)} %all-gather.3.cloned.1.call-done.down_ref) | copy-start | bytes 39321604
  239.5 1.7 copy-start.3
Sparse Core Ops, SparseCore 0:
  10.2 119.4 all-gather.4
  132.6 102.0 all-gather.2
